TPU v7x, 256 devices: a whole 4x4x8 slice. The times are simulated.
256 devices in a mesh: row: 32 (over z, y), col: 8 (over x, core).
Axes of the slice: x: 4, y: 4, z: 8, core: 2. Of those that a mesh axis runs over, the one named last changes fastest.
Arguments:
- momentum: float32 [5120, 9216], P('row', 'col'), may hold values from -300 to 300
- gradient: bfloat16 [5120, 9216], P('row', 'col'), may hold values from -300 to 300
Outputs:
- new_momentum: float32 [5120, 9216], P('row', 'col')
- update: float32 [5120, 9216], P('row', 'col')
All inputs are finite; a program needn't handle non-finite values.
Results may differ from a plain program's by a relative error of at most 0.0004.
The roundings to bfloat16 on the way count: a program that leaves them out, or rounds other values in their place, can miss the bound.
Values may be sent and summed in bfloat16 or wider, within the bound.
A program may use at most 128 MiB of HBM per device.

v0:
```python
import math

import jax
import jax.numpy as jnp
from jax import lax
from jax.sharding import PartitionSpec as P

decay_rate = 0.95
linear_coef = 3.4445
cubic_coef = -4.775
quintic_coef = 2.0315
norm_eps = 1e-07


def local(momentum, gradient):
    new_momentum = decay_rate * momentum + gradient.astype(jnp.float32)
    iterate = new_momentum.astype(jnp.bfloat16)
    wide_iterate = iterate.astype(jnp.float32)
    rows_here, cols_here = iterate.shape
    row_count = lax.axis_size("row")
    width_rows = rows_here * row_count
    width_cols = cols_here * lax.axis_size("col")
    own_sum = jnp.sum(wide_iterate * wide_iterate)
    norm_total = lax.psum(own_sum, ("row", "col"))
    gathered = lax.all_gather(iterate, "row", axis=0, tiled=True)
    partial_value = lax.dot_general(
        iterate, gathered, (((1,), (1,)), ((), ())), preferred_element_type=jnp.float32
    )
    gram_tile = lax.psum_scatter(partial_value, "col", scatter_dimension=1, tiled=True)
    tile_bf = gram_tile.astype(jnp.bfloat16)
    gram_panel = lax.all_gather(tile_bf, "col", axis=1, tiled=True)
    square = jnp.dot(
        gram_panel,
        lax.all_gather(tile_bf, "row", axis=0, tiled=True),
        preferred_element_type=jnp.float32,
    )
    factor = math.sqrt(width_rows) / (3.0 * (jnp.sqrt(norm_total) + norm_eps))
    polynom = (
        cubic_coef * factor * factor * tile_bf.astype(jnp.float32)
        + quintic_coef * factor**4 * square
    ).astype(jnp.bfloat16)
    product = jnp.dot(
        lax.all_gather(polynom, "col", axis=1, tiled=True),
        gathered,
        preferred_element_type=jnp.float32,
    )
    update = math.sqrt(width_cols) * factor * (linear_coef * wide_iterate + product)
    return (new_momentum, update)


def solution(mesh):
    placed = (P("row", "col"), P("row", "col"))
    return jax.shard_map(
        local,
        mesh=mesh,
        in_specs=placed,
        out_specs=(P("row", "col"), P("row", "col")),
        check_vma=False,
    )
```

profile of v0, /device:TPU:1, one launch (start us, length us, event | category | flops | bytes accessed | tf_op | source)
XLA Modules:
  0.0 342.5 jit_solution(13491634868362857029)
XLA Ops:
  7.2 0.0 all-gather.5.cloned.1.call-start
  7.2 2.9 fusion.3
  10.2 0.0 all-gather.5.cloned.1.call-update
  10.2 0.0 reduce-scatter.2.cloned.1.call-start
  10.2 120.1 %all-gather.5.cloned.1.call-done = bf16[5120,1152]{1,0:T(8,128)(2,1)} async-done(((bf16[160,1152]{1,0:T(8,128)(2,1)}), bf16[5120,1152]{1,0:T(8,128)(2,1)}) %all-gather.5.cloned.1.call-update) | async-done | bytes 11796496 | tf_op jit(solution)/shard_map/all_gather | solution.py:25
  130.4 10.2 %fusion.4 = f32[160,5120]{1,0:T(8,128)} fusion(bf16[160,1152]{1,0:T(8,128)(2,1)} %get-tuple-element.3, bf16[5120,1152]{1,0:T(8,128)(2,1)} %all-gather.5.cloned.1.call-done), kind=kOutput, calls=%fused_computation.9 | convolution fusion | flops 1887436800 | bytes 15441920 | tf_op jit(solution)/shard_map/dot_general | solution.py:26
  140.5 0.0 reduce-scatter.2.cloned.1.call-update
  140.6 0.0 all-gather.7.cloned.1.call-start
  140.6 33.3 %reduce-scatter.2.cloned.1.call-done = f32[160,640]{1,0:T(8,128)} async-done(((f32[160,5120]{1,0:T(8,128)}), f32[160,640]{1,0:T(8,128)}) %reduce-scatter.2.cloned.1.call-update) | async-done | bytes 409616 | tf_op jit(solution)/shard_map/reduce_scatter | solution.py:29
  173.9 1.7 convert_element_type.21
  175.6 0.0 all-gather.7.cloned.1.call-update
  175.7 0.0 all-gather.9.cloned.1.call-start
  175.7 0.5 all-gather.9.cloned.1.call-update
  176.2 0.0 all-gather.11.cloned.1.call-start
  176.3 79.3 %psum.7 = f32[]{:T(128)} all-reduce(f32[]{:T(128)} %get-tuple-element.2), channel_id=1, replica_groups=mesh['row'=32,'col'=8] {'row','col'}, use_global_device_ids=true, to_apply=%region_1.0 | all-reduce | flops 1 | bytes 8 | tf_op jit(solution)/shard_map/psum | solution.py:24
  256.3 0.0 copy-start
  256.3 0.0 all-gather.7.cloned.1.call-done
  256.3 40.9 %all-gather.9.cloned.1.call-done = bf16[5120,640]{1,0:T(8,128)(2,1)} async-done(((bf16[160,640]{1,0:T(8,128)(2,1)}), bf16[5120,640]{1,0:T(8,128)(2,1)}) %all-gather.9.cloned.1.call-update) | async-done | bytes 6553616 | tf_op jit(solution)/shard_map/all_gather | solution.py:34
  297.2 5.4 %fusion.2 = bf16[160,640]{1,0:T(8,128)(2,1)} fusion(bf16[160,5120]{1,0:T(8,128)(2,1)} %all-gather.7.cloned.1.call-done, bf16[5120,640]{1,0:T(8,128)(2,1)} %all-gather.9.cloned.1.call-done, bf16[160,640]{1,0:T(8,128)(2,1)} %convert_element_type.21, f32[]{:T(128)S(6)} %mul_shard_map.15, f32[]{:T(128)S(6)} %mul.48), kind=kOutput, calls=%fused_computation.4 | convolution fusion | flops 1049088000 | bytes 8601608 | tf_op jit(solution)/shard_map/dot_general | solution.py:32
  302.6 0.0 all-gather.11.cloned.1.call-update
  302.7 25.2 %all-gather.11.cloned.1.call-done = bf16[160,5120]{1,0:T(8,128)(2,1)} async-done(((bf16[160,640]{1,0:T(8,128)(2,1)}), bf16[160,5120]{1,0:T(8,128)(2,1)}) %all-gather.11.cloned.1.call-update) | async-done | bytes 1638416 | tf_op jit(solution)/shard_map/all_gather | solution.py:43
  327.9 0.0 copy-done
  327.9 8.0 %fusion = f32[160,1152]{1,0:T(8,128)} fusion(bf16[160,5120]{1,0:T(8,128)(2,1)} %all-gather.11.cloned.1.call-done, bf16[5120,1152]{1,0:T(8,128)(2,1)} %all-gather.5.cloned.1.call-done, bf16[160,1152]{1,0:T(8,128)(2,1)S(1)} %copy-done, f32[]{:T(128)S(6)} %mul_shard_map.13), kind=kOutput, calls=%fused_computation.1 | convolution fusion | flops 1888174080 | bytes 14540804 | tf_op jit(solution)/shard_map/dot_general | solution.py:42
Async XLA Ops:
  7.2 123.2 %all-gather.5.cloned.1.call-start = ((), (), s32[]{:S(2)}) async-start(), calls=%async_computation.1 | async-start | bytes 12165120 | tf_op jit(solution)/shard_map/all_gather | solution.py:25
  10.2 163.7 %reduce-scatter.2.cloned.1.call-start = ((), (), s32[]{:S(2)}) async-start(), calls=%async_computation.2 | async-start | bytes 3686400 | tf_op jit(solution)/shard_map/reduce_scatter | solution.py:29
  140.6 115.7 %all-gather.7.cloned.1.call-start = ((), (), s32[]{:S(2)}) async-start(), calls=%async_computation.3 | async-start | bytes 1843200 | tf_op jit(solution)/shard_map/all_gather | solution.py:31
  175.7 121.5 %all-gather.9.cloned.1.call-start = ((), (), s32[]{:S(2)}) async-start(), calls=%async_computation.4 | async-start | bytes 6758400 | tf_op jit(solution)/shard_map/all_gather | solution.py:34
  176.2 151.7 %all-gather.11.cloned.1.call-start = ((), (), s32[]{:S(2)}) async-start(), calls=%async_computation.5 | async-start | bytes 1843200 | tf_op jit(solution)/shard_map/all_gather | solution.py:43
  256.3 71.7 %copy-start = (bf16[160,1152]{1,0:T(8,128)(2,1)S(1)}, bf16[160,1152]{1,0:T(8,128)(2,1)}, u32[]{:S(2)}) copy-start(bf16[160,1152]{1,0:T(8,128)(2,1)} %get-tuple-element.3) | copy-start | bytes 1105924
Sparse Core Ops, SparseCore 0:
  11.1 119.1 all-gather.4
  140.7 33.1 reduce-scatter.1
  175.9 29.3 all-gather.6
  208.1 89.0 all-gather.8
  302.8 25.0 all-gather.10
where the time goes:
time: 343 us; the launch traced here: 342 us
  waiting for transfers between devices  220 us (64%)
  blocking collectives  79.3 us (23%)
  matrix products  23.7 us (7%)
  between operations  14.4 us (4%)
  other arithmetic  4.65 us (1%)
    all_gather x1, waiting for transfers between devices, local(): gathered = lax.all_gather(iterate, 'row', axis=0, tiled=True)  120 us
    psum x1, blocking collectives, local(): norm_total = lax.psum(own_sum, ('row', 'col'))  79.3 us
    all_gather x1, waiting for transfers between devices, local(): lax.all_gather(tile_bf, 'row', axis=0, tiled=True)  40.9 us
    reduce_scatter x1, waiting for transfers between devices, local(): lax.psum_scatter(partial_value, 'col', scatter_dimension=1, tiled=True)  33.3 us
    all_gather x1, waiting for transfers between devices, local(): lax.all_gather(polynom, 'col', axis=1, tiled=True)  25.2 us
    dot_general x1, matrix products, local(): lax.dot_general(iterate, gathered, (((1,), (1,)), ((), ())), preferred_el...  10.2 us
    dot_general x1, matrix products, local(): jnp.dot(lax.all_gather(polynom, 'col', axis=1, tiled=True), gathered, pre...  8.03 us
  transfers between devices with their start and end apart: 5, of which 4 were waited for; matrix products, arithmetic and copies ran while one was open for 0% of the time, Pallas kernels for 0%

commit v1 on v0

v1 whole, which is shorter than its diff:
```python
import math

import jax
import jax.numpy as jnp
from jax import lax
from jax.sharding import PartitionSpec as P

decay_rate = 0.95
linear_coef = 3.4445
cubic_coef = -4.775
quintic_coef = 2.0315
norm_eps = 1e-07

Y = 4
Z = 8


def local(momentum, gradient):
    new_momentum = decay_rate * momentum + gradient.astype(jnp.float32)
    iterate = new_momentum.astype(jnp.bfloat16)
    wide_iterate = iterate.astype(jnp.float32)
    rows_here, cols_here = iterate.shape
    width_rows = rows_here * lax.axis_size("row")
    width_cols = cols_here * lax.axis_size("col")
    along_y = [[z * Y + y for y in range(Y)] for z in range(Z)]
    along_z = [[z * Y + y for z in range(Z)] for y in range(Y)]
    norm_total = lax.psum(jnp.sum(wide_iterate * wide_iterate), ("row", "col"))
    rows_z = lax.all_gather(iterate, "row", axis=0, tiled=True, axis_index_groups=along_y)
    rows_y = lax.all_gather(iterate, "row", axis=0, tiled=True, axis_index_groups=along_z)
    partial_gram = lax.dot_general(
        rows_y, rows_z, (((1,), (1,)), ((), ())), preferred_element_type=jnp.float32
    )
    tile = lax.psum_scatter(partial_gram, "col", scatter_dimension=0, tiled=True)
    tile_bf = tile.astype(jnp.bfloat16)
    panel = lax.all_gather(tile_bf, "row", axis=1, tiled=True, axis_index_groups=along_z)
    column = lax.all_gather(tile_bf, "row", axis=0, axis_index_groups=along_y)
    column = lax.all_gather(column, "col", axis=0)
    column = column.reshape(width_rows, tile.shape[1])
    square = jnp.dot(panel, column, preferred_element_type=jnp.float32)
    factor = math.sqrt(width_rows) / (3.0 * (jnp.sqrt(norm_total) + norm_eps))
    polynom = (
        cubic_coef * factor * factor * tile_bf.astype(jnp.float32)
        + quintic_coef * factor**4 * square
    ).astype(jnp.bfloat16)
    wide_polynom = lax.all_gather(polynom, "col", axis=0, tiled=True)
    partial_product = lax.dot_general(
        wide_polynom, rows_y, (((0,), (0,)), ((), ())), preferred_element_type=jnp.float32
    )
    product = lax.psum_scatter(
        partial_product, "row", scatter_dimension=0, tiled=True, axis_index_groups=along_y
    )
    update = math.sqrt(width_cols) * factor * (linear_coef * wide_iterate + product)
    return (new_momentum, update)


def solution(mesh):
    placed = (P("row", "col"), P("row", "col"))
    return jax.shard_map(
        local,
        mesh=mesh,
        in_specs=placed,
        out_specs=(P("row", "col"), P("row", "col")),
        check_vma=False,
    )
```

time: 343 us -> 310 us (0.904)
  waiting for transfers between devices: 220 us -> 177 us
  blocking collectives: 79.3 us -> 93.7 us
  matrix products: 23.7 us -> 17.6 us
    all_gather x4 -> x5, waiting for transfers between devices: 186 us -> 101 us  [the longest x2 76.7 us: local(): lax.all_gather(iterate, 'row', axis=0, tiled=True, axis_index_groups=alon...]
    reduce_scatter x1 -> x2, waiting for transfers between devices: 33.3 us -> 75.2 us  [the longest x1 39.3 us: local(): lax.psum_scatter(partial_product, 'row', scatter_dimension=0, tiled=True,...]
    all_gather x0 -> x1, blocking collectives: none -> 13.1 us  [local(): column = lax.all_gather(tile_bf, 'row', axis=0, axis_index_groups=along_y)]
    dot_general x3, matrix products: 23.7 us -> 17.6 us  [the longest x1 6.63 us: local(): lax.dot_general(rows_y, rows_z, (((1,), (1,)), ((), ())), preferred_eleme...]
  transfers between devices with their start and end apart: 5 -> 7, of which waited for: 4 -> 5; matrix products, arithmetic and copies ran while one was open for 0% -> 0% of each run, Pallas kernels for 0% -> 0%
where the time goes in v1:
time: 310 us
  waiting for transfers between devices  177 us (57%)
  blocking collectives  93.7 us (30%)
  matrix products  17.6 us (6%)
  between operations  14.8 us (5%)
  other arithmetic  6.79 us (2%)
    psum x1, blocking collectives, local(): norm_total = lax.psum(jnp.sum(wide_iterate * wide_iterate), ('row', 'col'))  80.6 us
    all_gather x2, waiting for transfers between devices, local(): lax.all_gather(iterate, 'row', axis=0, tiled=True, axis_index_groups=alon...  76.7 us
    reduce_scatter x1, waiting for transfers between devices, local(): lax.psum_scatter(partial_product, 'row', scatter_dimension=0, tiled=True,...  39.3 us
    reduce_scatter x1, waiting for transfers between devices, local(): lax.psum_scatter(partial_gram, 'col', scatter_dimension=0, tiled=True)  35.9 us
    all_gather x1, waiting for transfers between devices, local(): wide_polynom = lax.all_gather(polynom, 'col', axis=0, tiled=True)  24.1 us
    all_gather x1, blocking collectives, local(): column = lax.all_gather(tile_bf, 'row', axis=0, axis_index_groups=along_y)  13.1 us
    dot_general x1, matrix products, local(): lax.dot_general(rows_y, rows_z, (((1,), (1,)), ((), ())), preferred_eleme...  6.63 us
  transfers between devices with their start and end apart: 7, of which 5 were waited for; matrix products, arithmetic and copies ran while one was open for 0% of the time, Pallas kernels for 0%

profile of v1, /device:TPU:1, one launch (start us, length us, event | category | flops | bytes accessed | tf_op | source)
XLA Modules:
  0.0 310.1 jit_solution(8542790231907557781)
XLA Ops:
  7.2 0.0 all-gather.10.cloned.1.call-start
  7.2 3.0 fusion.2
  10.2 0.0 all-gather.10.cloned.1.call-update
  10.2 0.0 all-gather.8.cloned.1.call-start
  10.3 0.7 all-gather.8.cloned.1.call-update
  11.0 0.0 reduce-scatter.3.cloned.1.call-start
  11.0 31.4 %all-gather.10.cloned.1.call-done = bf16[640,1152]{1,0:T(8,128)(2,1)} async-done(((bf16[160,1152]{1,0:T(8,128)(2,1)}), bf16[640,1152]{1,0:T(8,128)(2,1)}) %all-gather.10.cloned.1.call-update) | async-done | bytes 1474576 | tf_op jit(solution)/shard_map/all_gather | solution.py:28
  42.4 45.3 %all-gather.8.cloned.1.call-done = bf16[1280,1152]{1,0:T(8,128)(2,1)} async-done(((bf16[160,1152]{1,0:T(8,128)(2,1)}), bf16[1280,1152]{1,0:T(8,128)(2,1)}) %all-gather.8.cloned.1.call-update) | async-done | bytes 2949136 | tf_op jit(solution)/shard_map/all_gather | solution.py:29
  87.8 6.6 %fusion.5 = f32[1280,640]{1,0:T(8,128)} fusion(bf16[1280,1152]{1,0:T(8,128)(2,1)} %all-gather.8.cloned.1.call-done, bf16[640,1152]{1,0:T(8,128)(2,1)} %all-gather.10.cloned.1.call-done), kind=kOutput, calls=%fused_computation.9 | convolution fusion | flops 1887436800 | bytes 7700480 | tf_op jit(solution)/shard_map/dot_general | solution.py:30
  94.4 0.0 reduce-scatter.3.cloned.1.call-update
  94.4 0.0 all-gather.12.cloned.1.call-start
  94.5 35.9 %reduce-scatter.3.cloned.1.call-done = f32[160,640]{1,0:T(8,128)} async-done(((f32[1280,640]{1,0:T(8,128)}), f32[160,640]{1,0:T(8,128)}) %reduce-scatter.3.cloned.1.call-update) | async-done | bytes 409616 | tf_op jit(solution)/shard_map/reduce_scatter | solution.py:33
  130.4 1.7 convert_element_type.21
  132.1 0.0 all-gather.12.cloned.1.call-update
  132.1 0.0 all-gather.16.cloned.1.call-start
  132.2 13.1 %all-gather = bf16[640,640]{1,0:T(8,128)(2,1)} all-gather(bf16[160,640]{1,0:T(8,128)(2,1)} %convert_element_type.21), channel_id=2, replica_groups={{0,8,16,24},{32,40,48,56},{64,72,80,88},{96,104,112,120},{128,136,144,1..., dimensions={0}, use_global_device_ids=true | all-gather | bytes 1024000 | tf_op jit(solution)/shard_map/all_gather | solution.py:36
  145.3 0.0 all-gather.16.cloned.1.call-update
  145.3 0.0 all-gather.14.cloned.1.call-start
  145.4 80.6 %psum.7 = f32[]{:T(128)} all-reduce(f32[]{:T(128)} %get-tuple-element.2), channel_id=1, replica_groups=mesh['row'=32,'col'=8] {'row','col'}, use_global_device_ids=true, to_apply=%region_1.0 | all-reduce | flops 1 | bytes 8 | tf_op jit(solution)/shard_map/psum | solution.py:27
  226.7 0.0 all-gather.12.cloned.1.call-done
  226.7 0.0 all-gather.16.cloned.1.call-done
  226.7 0.0 copy-start.1
  226.7 5.6 %fusion.1 = bf16[160,640]{1,0:T(8,128)(2,1)} fusion(bf16[160,5120]{1,0:T(8,128)(2,1)} %all-gather.12.cloned.1.call-done, bf16[5120,640]{1,0:T(8,128)(2,1)} %bitcast.8, bf16[160,640]{1,0:T(8,128)(2,1)} %convert_element_type.21, f32[]{:T(128)S(6)} %mul_shard_map.15, f32[]{:T(128)S(6)} %mul.48), kind=kOutput, calls=%fused_computation.2 | convolution fusion | flops 1049088000 | bytes 8601608 | tf_op jit(solution)/shard_map/dot_general | solution.py:39
  232.3 0.0 all-gather.14.cloned.1.call-update
  232.3 0.0 reduce-scatter.5.cloned.1.call-start
  232.4 24.1 %all-gather.14.cloned.1.call-done = bf16[1280,640]{1,0:T(8,128)(2,1)} async-done(((bf16[160,640]{1,0:T(8,128)(2,1)}), bf16[1280,640]{1,0:T(8,128)(2,1)}) %all-gather.14.cloned.1.call-update) | async-done | bytes 1638416 | tf_op jit(solution)/shard_map/all_gather | solution.py:45
  256.5 0.0 copy-done.1
  256.5 5.4 %fusion.6 = f32[640,1152]{1,0:T(8,128)} fusion(bf16[1280,640]{1,0:T(8,128)(2,1)} %all-gather.14.cloned.1.call-done, bf16[1280,1152]{1,0:T(8,128)(2,1)S(1)} %copy-done.1), kind=kOutput, calls=%fused_computation.10 | convolution fusion | flops 1887436800 | bytes 7536640 | tf_op jit(solution)/shard_map/dot_general | solution.py:46
  261.9 0.0 reduce-scatter.5.cloned.1.call-update
  261.9 39.3 %reduce-scatter.5.cloned.1.call-done = f32[160,1152]{1,0:T(8,128)} async-done(((f32[640,1152]{1,0:T(8,128)}), f32[160,1152]{1,0:T(8,128)}) %reduce-scatter.5.cloned.1.call-update) | async-done | bytes 737296 | tf_op jit(solution)/shard_map/reduce_scatter | solution.py:49
  301.2 0.0 copy-done
  301.2 2.1 fusion.4
  (1 shorter events, 0.0 us)
Async XLA Ops:
  7.2 35.3 %all-gather.10.cloned.1.call-start = ((), (), s32[]{:S(2)}) async-start(), calls=%async_computation.3 | async-start | bytes 1843200 | tf_op jit(solution)/shard_map/all_gather | solution.py:28
  10.2 77.5 %all-gather.8.cloned.1.call-start = ((), (), s32[]{:S(2)}) async-start(), calls=%async_computation.2 | async-start | bytes 3317760 | tf_op jit(solution)/shard_map/all_gather | solution.py:29
  11.0 119.4 %reduce-scatter.3.cloned.1.call-start = ((), (), s32[]{:S(2)}) async-start(), calls=%async_computation.4 | async-start | bytes 3686400 | tf_op jit(solution)/shard_map/reduce_scatter | solution.py:33
  94.4 132.2 %all-gather.12.cloned.1.call-start = ((), (), s32[]{:S(2)}) async-start(), calls=%async_computation.5 | async-start | bytes 1843200 | tf_op jit(solution)/shard_map/all_gather | solution.py:35
  132.1 94.6 %all-gather.16.cloned.1.call-start = ((), (), s32[]{:S(2)}) async-start(), calls=%async_computation.8 | async-start | bytes 7372800 | tf_op jit(solution)/shard_map/all_gather | solution.py:37
  145.3 111.2 %all-gather.14.cloned.1.call-start = ((), (), s32[]{:S(2)}) async-start(), calls=%async_computation.6 | async-start | bytes 1843200 | tf_op jit(solution)/shard_map/all_gather | solution.py:45
  226.7 29.8 %copy-start.1 = (bf16[1280,1152]{1,0:T(8,128)(2,1)S(1)}, bf16[1280,1152]{1,0:T(8,128)(2,1)}, u32[]{:S(2)}) copy-start(bf16[1280,1152]{1,0:T(8,128)(2,1)} %all-gather.8.cloned.1.call-done) | copy-start | bytes 8847364
  232.3 68.9 %reduce-scatter.5.cloned.1.call-start = ((), (), s32[]{:S(2)}) async-start(), calls=%async_computation.7 | async-start | bytes 3686400 | tf_op jit(solution)/shard_map/reduce_scatter | solution.py:49
  261.9 39.3 %copy-start = (bf16[160,1152]{1,0:T(8,128)(2,1)S(1)}, bf16[160,1152]{1,0:T(8,128)(2,1)}, u32[]{:S(2)}) copy-start(bf16[160,1152]{1,0:T(8,128)(2,1)} %get-tuple-element.3) | copy-start | bytes 1105924
Sparse Core Ops, SparseCore 0:
  10.4 32.0 all-gather.9
  44.8 42.9 all-gather.7
  94.5 35.8 reduce-scatter.2
  132.3 37.2 all-gather.11
  171.3 48.0 all-gather.15
  232.5 24.0 all-gather.13
  262.1 39.1 reduce-scatter.4

commit v2 on v0

v2 whole, which is shorter than its diff:
```python
import math

import jax
import jax.numpy as jnp
from jax import lax
from jax.experimental import pallas as pl
from jax.experimental.pallas import tpu as pltpu
from jax.sharding import PartitionSpec as P

decay_rate = 0.95
linear_coef = 3.4445
cubic_coef = -4.775
quintic_coef = 2.0315
norm_eps = 1e-07

X, Y, Z = 4, 4, 8
ROWS, COLS = 160, 1152
HALF = ROWS // 2
WIDE = Y * ROWS
TILES = 3
TILE = COLS // TILES
FULL_ROWS = ROWS * Y * Z
FULL_COLS = COLS * X * 2
NT = (((1,), (1,)), ((), ()))
TN = (((0,), (0,)), ((), ()))
F32 = jnp.float32
BF16 = jnp.bfloat16


def wrap(value, size):
    return lax.rem(value + size, size)


def remote(src, dst, send_sem, recv_sem, device):
    return pltpu.make_async_remote_copy(
        src_ref=src,
        dst_ref=dst,
        send_sem=send_sem,
        recv_sem=recv_sem,
        device_id=device,
        device_id_type=pl.DeviceIdType.MESH,
    )


class Ring:
    def __init__(self, size, position, device, region, last, send_sems, recv_sems):
        self.size, self.position, self.device = size, position, device
        self.region, self.last = region, last
        self.send_sems, self.recv_sems = send_sems, recv_sems

    def steps(self, way, piece):
        return self.size // 2 - (0 if self.last[piece] == way else 1)

    def copy(self, way, step, piece, block):
        sign = 1 - 2 * way
        place = self.region(block, piece)
        return remote(
            place,
            place,
            self.send_sems.at[way, step, piece],
            self.recv_sems.at[way, step, piece],
            self.device(wrap(self.position + sign, self.size)),
        )

    def send(self, way, step, piece):
        sign = 1 - 2 * way
        self.copy(way, step, piece, wrap(self.position - sign * step, self.size)).start()

    def start(self, piece):
        for way in (0, 1):
            self.send(way, 0, piece)

    def recv(self, way, step, piece):
        if step >= self.steps(way, piece):
            return
        sign = 1 - 2 * way
        self.copy(way, step, piece, wrap(self.position - sign * (step + 1), self.size)).wait_recv()
        if step + 1 < self.steps(way, piece):
            self.send(way, step + 1, piece)

    def finish(self):
        for way in (0, 1):
            for piece in range(len(self.last)):
                for step in range(self.steps(way, piece)):
                    sign = 1 - 2 * way
                    self.copy(way, step, piece, wrap(self.position - sign * step, self.size)).wait_send()


OFFSETS = (0, 1, -1, 2, -2, 3, -3, 4)


def kernel(
    iterate,
    product,
    factor_out,
    xa, xb, part, sibling_part, relay, last_part, gj, gall, pb, up, y_relay, y_last,
    square, ss_z, ss_y, ss_x, ss_c,
    zr_s, zr_r, yr_s, yr_r, sp_s, sp_r, rl_s, rl_r, lp_s, lp_r,
    gz_s, gz_r, gx0_s, gx0_r, gy0_s, gy0_r, gy1_s, gy1_r, gx1_s, gx1_r, gs_s, gs_r,
    pr_s, pr_r, ps_s, ps_r, ssy_s, ssy_r, ssx_s, ssx_r, ssc_s, ssc_r,
    ur_s, ur_r, ul_s, ul_r,
):
    row, col = lax.axis_index("row"), lax.axis_index("col")
    z, y = lax.div(row, Y), lax.rem(row, Y)
    x, core = lax.div(col, 2), lax.rem(col, 2)
    other = 1 - core

    def at_z(p):
        return (p * Y + y, col)

    def at_y(p):
        return (z * Y + p, col)

    def at_x(p):
        return (row, p * 2 + core)

    sibling = (row, x * 2 + other)

    barrier = pltpu.get_barrier_semaphore()
    partners = [at_z(wrap(z + 1, Z)), at_z(wrap(z - 1, Z)), sibling]
    partners += [at_y(wrap(y + d, Y)) for d in (1, 2, 3)]
    partners += [at_x(wrap(x + d, X)) for d in (1, 2, 3)]
    for partner in partners:
        pl.semaphore_signal(barrier, inc=1, device_id=partner, device_id_type=pl.DeviceIdType.MESH)
    xb[z] = iterate[...]
    xa[y] = iterate[...]
    pl.semaphore_wait(barrier, len(partners))

    zr = Ring(Z, z, at_z, lambda b, p: xb.at[b, pl.ds(p * HALF, HALF)], (0, 1), zr_s, zr_r)
    yr = Ring(Y, y, at_y, lambda b, p: xa.at[b, pl.ds(p * HALF, HALF)], (0, 1), yr_s, yr_r)
    for way, piece in ((0, 0), (1, 1), (0, 1), (1, 0)):
        zr.send(way, 0, piece)
        yr.send(way, 0, piece)

    def z_of(event):
        return wrap(z + OFFSETS[event], Z)

    def sibling_copy(there):
        return remote(
            part.at[there, other], sibling_part.at[there], sp_s.at[there], sp_r.at[there], sibling
        )

    def form(event):
        there = z_of(event)
        block = xb[there]
        part[there] = lax.dot_general(
            block, xa[...].reshape(WIDE, COLS), NT, preferred_element_type=F32
        ).reshape(2, HALF, WIDE)
        sibling_copy(there).start()
        wide = block.astype(F32)
        ss_z[there] = jnp.broadcast_to(jnp.sum(wide * wide, keepdims=True), (8, 128))

    def role_of(there):
        return wrap(x - lax.div(there, 2), X)

    def relay_copy(there, side):
        place = pl.ds(side * (HALF // 2), HALF // 2)
        return remote(
            part.at[there, core, place],
            relay.at[there],
            rl_s.at[there, side],
            rl_r.at[there],
            at_x(wrap(x - 1 + 2 * side, X)),
        )

    def last_copy(there, role):
        side = lax.div(role, 2)
        half = lax.rem(there, 2)
        return remote(
            part.at[there, core],
            last_part.at[half, side],
            lp_s.at[there],
            lp_r.at[half, side],
            at_x(wrap(x + role - 2, X)),
        )

    def join(event):
        there = z_of(event)
        sibling_copy(there).wait_recv()
        part[there, core] = part[there, core] + sibling_part[there]

        @pl.when(role_of(there) == 2)
        def _():
            relay_copy(there, 0).start()
            relay_copy(there, 1).start()

    def pass_on(event):
        there = z_of(event)
        role = role_of(there)

        @pl.when(lax.rem(role, 2) == 1)
        def _():
            relay_copy(there, 0).wait_recv()
            place = pl.ds(pl.multiple_of(lax.div(role, 2) * (HALF // 2), 8), HALF // 2)
            part[there, core, place] = part[there, core, place] + relay[there]
            last_copy(there, role).start()

    def z_step(step):
        for way, piece in ((0, 0), (1, 1), (0, 1), (1, 0)):
            zr.recv(way, step, piece)

    z_step(0)
    for step in (0, 1):
        for way, piece in ((0, 0), (1, 1), (0, 1), (1, 0)):
            yr.recv(way, step, piece)
    form(0)
    form(1)
    form(2)
    join(0)
    join(1)
    join(2)
    z_step(1)
    form(3)
    form(4)
    pass_on(0)
    pass_on(1)
    pass_on(2)
    join(3)
    join(4)
    z_step(2)
    form(5)
    form(6)
    pass_on(3)
    pass_on(4)
    join(5)
    join(6)
    z_step(3)
    form(7)
    pass_on(5)
    pass_on(6)
    join(7)
    pass_on(7)

    def small(refs, slot, send_sems, recv_sems, index, device):
        return remote(refs.at[slot], refs.at[slot], send_sems.at[index], recv_sems.at[index], device)

    total = ss_z[0]
    for k in range(1, Z):
        total = total + ss_z[k]
    ss_y[y] = total
    for d in (1, 2, 3):
        small(ss_y, y, ssy_s, ssy_r, d - 1, at_y(wrap(y + d, Y))).start()

    gz = Ring(Z, z, at_z, lambda b, p: gj.at[b, p], (0, 1), gz_s, gz_r)
    cut = ((0, 48), (48, 32))
    gx0 = Ring(X, x, at_x, lambda b, p: gall.at[b, 0, y, core, pl.ds(*cut[p])], (0, 1), gx0_s, gx0_r)
    gy0 = Ring(Y, y, at_y, lambda b, p: gall.at[wrap(x + p, X), 0, b, core], (0, 0, 1, 1), gy0_s, gy0_r)
    gy1 = Ring(Y, y, at_y, lambda b, p: gall.at[x, 1, b, core, pl.ds(*cut[p])], (0, 1), gy1_s, gy1_r)
    gx1 = Ring(X, x, at_x, lambda b, p: gall.at[b, 1, wrap(y + p, Y), core], (0, 0, 1, 1), gx1_s, gx1_r)

    def last_wait(half, side):
        there = 2 * x + half
        remote(
            part.at[there, core], last_part.at[half, side], lp_s.at[there], lp_r.at[half, side], sibling
        ).wait_recv()

    def settle(half):
        last_wait(half, 0)
        last_wait(half, 1)
        tile = (part[2 * x + half, core] + last_part[half, 0] + last_part[half, 1]).astype(BF16)
        gj[z, half] = tile
        gall[x, half, y, core] = tile

    settle(0)
    gx0.start(0)
    gx0.start(1)
    gz.start(0)
    gy0.start(0)
    settle(1)
    gy1.start(0)
    gy1.start(1)
    gz.start(1)
    gx1.start(0)

    for d in (1, 2, 3):
        small(ss_y, wrap(y - d, Y), ssy_s, ssy_r, d - 1, sibling).wait_recv()
    ss_x[x] = ss_y[0] + ss_y[1] + ss_y[2] + ss_y[3]
    for d in (1, 2, 3):
        small(ss_x, x, ssx_s, ssx_r, d - 1, at_x(wrap(x + d, X))).start()

    four = ((0, 0), (1, 1), (0, 1), (1, 0))

    def both(ring, step, pieces):
        for piece in pieces:
            ring.recv(0, step, piece)
            ring.recv(1, step, piece)

    def share(half, index, core_):
        if half == 0:
            place = gall.at[:, 0, wrap(y + index, Y), core_]
        else:
            place = gall.at[wrap(x + index, X), 1, :, core_]
        return remote(place, place, gs_s.at[half, index], gs_r.at[half, index], sibling)

    for way, piece in four:
        gx0.recv(way, 0, piece)
    gy0.start(1)
    gy0.start(3)
    for way, piece in four:
        gy1.recv(way, 0, piece)
    gx1.start(1)
    gx1.start(3)
    both(gz, 0, (0, 1))
    for way, piece in four:
        gx0.recv(way, 1, piece)
    gy0.start(2)
    for way, piece in four:
        gy1.recv(way, 1, piece)
    gx1.start(2)
    share(0, 0, core).start()
    share(1, 0, core).start()

    for d in (1, 2, 3):
        small(ss_x, wrap(x - d, X), ssx_s, ssx_r, d - 1, sibling).wait_recv()
    ss_c[core] = ss_x[0] + ss_x[1] + ss_x[2] + ss_x[3]
    small(ss_c, core, ssc_s, ssc_r, 0, sibling).start()

    both(gy0, 0, (0,))
    both(gx1, 0, (0,))
    both(gz, 1, (0, 1))
    both(gy0, 0, (1, 3))
    both(gx1, 0, (1, 3))
    both(gz, 2, (0, 1))
    both(gy0, 0, (2,))
    both(gx1, 0, (2,))
    for index in (1, 3):
        share(0, index, core).start()
        share(1, index, core).start()
    both(gz, 3, (0, 1))
    both(gy0, 1, (0, 1, 2, 3))
    both(gx1, 1, (0, 1, 2, 3))
    share(0, 2, core).start()
    share(1, 2, core).start()
    small(ss_c, other, ssc_s, ssc_r, 0, sibling).wait_recv()
    norm_total = (ss_c[0] + ss_c[1])[0:1, 0:1]
    factor = math.sqrt(FULL_ROWS) / (3.0 * (jnp.sqrt(norm_total) + norm_eps))
    factor_out[...] = jnp.broadcast_to(factor, (8, 128))
    for index in (0, 1, 3, 2):
        share(0, index, other).wait_recv()
        share(1, index, other).wait_recv()

    square[...] = jnp.zeros_like(square)

    @pl.loop(0, Z)
    def _(there):
        square[...] += jnp.dot(
            gj[there].reshape(ROWS, WIDE),
            gall[lax.div(there, 2), lax.rem(there, 2)].reshape(WIDE, WIDE),
            preferred_element_type=F32,
        )

    pr = Ring(X, x, at_x, lambda b, p: pb.at[b, p, core], (0, 1), pr_s, pr_r)
    for half in (0, 1):
        gram = gj[z, half].astype(F32)
        tile = (
            cubic_coef * factor * factor * gram
            + quintic_coef * (factor * factor) * (factor * factor) * square[pl.ds(half * HALF, HALF)]
        )
        pb[x, half, core] = tile.astype(BF16)
        pr.start(half)

    def share_p(index, core_):
        place = pb.at[wrap(x + index, X), :, core_]
        return remote(place, place, ps_s.at[index], ps_r.at[index], sibling)

    share_p(0, core).start()
    for way, piece in four:
        pr.recv(way, 0, piece)
    share_p(1, core).start()
    share_p(3, core).start()
    for way, piece in four:
        pr.recv(way, 1, piece)
    share_p(2, core).start()
    for index in (0, 1, 3, 2):
        share_p(index, other).wait_recv()

    def y_relay_copy(tile, side):
        return remote(
            up.at[tile, wrap(y + 2, Y), pl.ds(side * HALF, HALF)],
            y_relay.at[tile, side],
            ur_s.at[tile, side],
            ur_r.at[tile, side],
            at_y(wrap(y + 1 - 2 * side, Y)),
        )

    def y_last_copy(tile, side, half):
        return remote(
            up.at[tile, wrap(y + 1 - 2 * side, Y), pl.ds(half * HALF, HALF)],
            y_last.at[tile, side, pl.ds(half * HALF, HALF)],
            ul_s.at[tile, side, half],
            ul_r.at[tile, side, half],
            at_y(wrap(y + 1 - 2 * side, Y)),
        )

    def add_relay(tile):
        for side in (0, 1):
            y_relay_copy(tile, side).wait_recv()
            near = wrap(y + 1 - 2 * side, Y)
            place = pl.ds(side * HALF, HALF)
            up[tile, near, place] = up[tile, near, place] + y_relay[tile, side]
            y_last_copy(tile, side, side).start()

    for tile in range(TILES):
        up[tile] = lax.dot_general(
            pb[...].reshape(Z * ROWS, WIDE),
            xb[:, :, pl.ds(tile * TILE, TILE)].reshape(Z * ROWS, TILE),
            TN,
            preferred_element_type=F32,
        ).reshape(Y, ROWS, TILE)
        for side in (0, 1):
            y_relay_copy(tile, side).start()
        for side in (0, 1):
            y_last_copy(tile, side, 1 - side).start()
    for tile in range(TILES):
        add_relay(tile)
    for tile in range(TILES):
        for side in (0, 1):
            for half in (0, 1):
                y_last_copy(tile, side, half).wait_recv()
        product[:, pl.ds(tile * TILE, TILE)] = up[tile, y] + y_last[tile, 0] + y_last[tile, 1]

    for ring in (zr, yr, gz, gx0, gy0, gy1, gx1, pr):
        ring.finish()
    for event in range(Z):
        there = z_of(event)
        sibling_copy(there).wait_send()
        role = role_of(there)

        @pl.when(role == 2)
        def _():
            relay_copy(there, 0).wait_send()
            relay_copy(there, 1).wait_send()

        @pl.when(lax.rem(role, 2) == 1)
        def _():
            last_copy(there, role).wait_send()

    for d in (1, 2, 3):
        small(ss_y, y, ssy_s, ssy_r, d - 1, sibling).wait_send()
        small(ss_x, x, ssx_s, ssx_r, d - 1, sibling).wait_send()
    small(ss_c, core, ssc_s, ssc_r, 0, sibling).wait_send()
    for index in range(4):
        share(0, index, core).wait_send()
        share(1, index, core).wait_send()
        share_p(index, core).wait_send()
    for tile in range(TILES):
        for side in (0, 1):
            y_relay_copy(tile, side).wait_send()
            for half in (0, 1):
                y_last_copy(tile, side, half).wait_send()


def dma(*shape):
    return pltpu.SemaphoreType.DMA(shape)


def twice(*shape):
    return [dma(*shape), dma(*shape)]


def fused(iterate):
    vmem = pl.BlockSpec(memory_space=pltpu.VMEM)
    return pl.pallas_call(
        kernel,
        out_shape=(
            jax.ShapeDtypeStruct((ROWS, COLS), F32),
            jax.ShapeDtypeStruct((8, 128), F32),
        ),
        in_specs=[vmem],
        out_specs=(vmem, vmem),
        scratch_shapes=[
            pltpu.VMEM((Y, ROWS, COLS), BF16),
            pltpu.VMEM((Z, ROWS, COLS), BF16),
            pltpu.VMEM((Z, 2, HALF, WIDE), F32),
            pltpu.VMEM((Z, HALF, WIDE), F32),
            pltpu.VMEM((Z, HALF // 2, WIDE), F32),
            pltpu.VMEM((2, 2, HALF, WIDE), F32),
            pltpu.VMEM((Z, 2, HALF, WIDE), BF16),
            pltpu.VMEM((X, 2, Y, 2, HALF, WIDE), BF16),
            pltpu.VMEM((X, 2, 2, HALF, WIDE), BF16),
            pltpu.VMEM((TILES, Y, ROWS, TILE), F32),
            pltpu.VMEM((TILES, 2, HALF, TILE), F32),
            pltpu.VMEM((TILES, 2, ROWS, TILE), F32),
            pltpu.VMEM((ROWS, WIDE), F32),
            pltpu.VMEM((Z, 8, 128), F32),
            pltpu.VMEM((Y, 8, 128), F32),
            pltpu.VMEM((X, 8, 128), F32),
            pltpu.VMEM((2, 8, 128), F32),
            *twice(2, 4, 2),
            *twice(2, 2, 2),
            *twice(Z),
            dma(Z, 2), dma(Z),
            dma(Z), dma(2, 2),
            *twice(2, 4, 2),
            *twice(2, 2, 2),
            *twice(2, 2, 4),
            *twice(2, 2, 2),
            *twice(2, 2, 4),
            *twice(2, 4),
            *twice(2, 2, 2),
            *twice(4),
            *twice(3),
            *twice(3),
            *twice(1),
            *twice(TILES, 2),
            *twice(TILES, 2, 2),
        ],
        compiler_params=pltpu.CompilerParams(
            collective_id=0, has_side_effects=True, vmem_limit_bytes=56 * 1024 * 1024
        ),
    )(iterate)


def local(momentum, gradient):
    new_momentum = decay_rate * momentum + gradient.astype(F32)
    iterate = new_momentum.astype(BF16)
    product, factor = fused(iterate)
    update = math.sqrt(FULL_COLS) * factor[0, 0] * (linear_coef * iterate.astype(F32) + product)
    return (new_momentum, update)


def solution(mesh):
    placed = (P("row", "col"), P("row", "col"))
    return jax.shard_map(
        local,
        mesh=mesh,
        in_specs=placed,
        out_specs=(P("row", "col"), P("row", "col")),
        check_vma=False,
    )
```

time: 343 us -> 139 us (0.41)
  waiting for transfers between devices: 220 us -> 0 us
  Pallas kernels: 0 us -> 132 us
  blocking collectives: 79.3 us -> 0 us
  matrix products: 23.7 us -> 0 us
  between operations: 14.4 us -> 1.2 us
    all_gather x4 -> x0, waiting for transfers between devices: 186 us -> none  [the longest x1 120 us: local(): gathered = lax.all_gather(iterate, 'row', axis=0, tiled=True)]
    pallas_call x0 -> x1, Pallas kernels: none -> 132 us  [fused(): pl.pallas_call(kernel, out_shape=(jax.ShapeDtypeStruct((ROWS, COLS), F32)...]
    psum x1 -> x0, blocking collectives: 79.3 us -> none  [local(): norm_total = lax.psum(own_sum, ('row', 'col'))]
    reduce_scatter x1 -> x0, waiting for transfers between devices: 33.3 us -> none  [local(): lax.psum_scatter(partial_value, 'col', scatter_dimension=1, tiled=True)]
    dot_general x3 -> x0, matrix products: 23.7 us -> none  [the longest x1 10.2 us: local(): lax.dot_general(iterate, gathered, (((1,), (1,)), ((), ())), preferred_el...]
  transfers between devices with their start and end apart: 5 -> 0, of which waited for: 4 -> 0; matrix products, arithmetic and copies ran while one was open for 0% -> 0% of each run, Pallas kernels for 0% -> 0%
where the time goes in v2:
time: 139 us
  Pallas kernels  132 us (95%)
  other arithmetic  4.38 us (3%)
    pallas_call x1, Pallas kernels, fused(): pl.pallas_call(kernel, out_shape=(jax.ShapeDtypeStruct((ROWS, COLS), F32)...  132 us

profile of v2, /device:TPU:1, one launch (start us, length us, event | category | flops | bytes accessed | tf_op | source)
XLA Modules:
  0.0 138.5 jit_solution(5586048770716223442)
XLA Ops:
  0.6 2.3 %fusion = (bf16[160,1152]{1,0:T(8,128)(2,1)}, f32[160,1152]{1,0:T(8,128)}) fusion(bf16[160,1152]{1,0:T(8,128)(2,1)} %param.3, f32[160,1152]{1,0:T(8,128)} %param.2), kind=kLoop, calls=%fused_computation.2 | loop fusion | flops 737280 | bytes 2211840 | tf_op jit(solution)/shard_map/convert_element_type | solution.py:516
  2.9 0.0 copy-start
  2.9 131.8 %shard_map.41 = (f32[160,1152]{1,0:T(8,128)}, f32[8,128]{1,0:T(8,128)}) custom-call(bf16[160,1152]{1,0:T(8,128)(2,1)} %get-tuple-element.6.iterate), custom_call_target="tpu_custom_call" | custom-call | tf_op jit(solution)/shard_map/pallas_call | solution.py:463
  134.7 1.2 slice.3
  136.4 0.0 copy-done
  136.5 2.1 %add_multiply_fusion = f32[160,1152]{1,0:T(8,128)} fusion(f32[160,1152]{1,0:T(8,128)} %get-tuple-element.5, bf16[160,1152]{1,0:T(8,128)(2,1)S(1)} %copy-done, f32[]{:T(128)} %bitcast), kind=kLoop, calls=%fused_computation | loop fusion | flops 737280 | bytes 1843204 | tf_op jit(solution)/shard_map/mul | solution.py:518
Async XLA Ops:
  2.9 133.5 %copy-start = (bf16[160,1152]{1,0:T(8,128)(2,1)S(1)}, bf16[160,1152]{1,0:T(8,128)(2,1)}, u32[]{:S(2)}) copy-start(bf16[160,1152]{1,0:T(8,128)(2,1)} %get-tuple-element.6.iterate) | copy-start | bytes 1105924

commit v3 on v2

--- a/solution.py
+++ b/solution.py
@@ -90,13 +90,14 @@
 
 
 def kernel(
-    iterate,
+    momentum,
+    gradient,
     product,
     factor_out,
     xa, xb, part, sibling_part, relay, last_part, gj, gall, pb, up, y_relay, y_last,
     square, ss_z, ss_y, ss_x, ss_c,
     zr_s, zr_r, yr_s, yr_r, sp_s, sp_r, rl_s, rl_r, lp_s, lp_r,
-    gz_s, gz_r, gx0_s, gx0_r, gy0_s, gy0_r, gy1_s, gy1_r, gx1_s, gx1_r, gs_s, gs_r,
+    gz_s, gz_r, gt_s, gt_r, gy_s, gy_r, gs_s, gs_r,
     pr_s, pr_r, ps_s, ps_r, ssy_s, ssy_r, ssx_s, ssx_r, ssc_s, ssc_r,
     ur_s, ur_r, ul_s, ul_r,
 ):
@@ -122,8 +123,9 @@
     partners += [at_x(wrap(x + d, X)) for d in (1, 2, 3)]
     for partner in partners:
         pl.semaphore_signal(barrier, inc=1, device_id=partner, device_id_type=pl.DeviceIdType.MESH)
-    xb[z] = iterate[...]
-    xa[y] = iterate[...]
+    iterate = (decay_rate * momentum[...] + gradient[...].astype(F32)).astype(BF16)
+    xb[z] = iterate
+    xa[y] = iterate
     pl.semaphore_wait(barrier, len(partners))
 
     zr = Ring(Z, z, at_z, lambda b, p: xb.at[b, pl.ds(p * HALF, HALF)], (0, 1), zr_s, zr_r)
@@ -151,7 +153,7 @@
         ss_z[there] = jnp.broadcast_to(jnp.sum(wide * wide, keepdims=True), (8, 128))
 
     def role_of(there):
-        return wrap(x - lax.div(there, 2), X)
+        return wrap(x - lax.rem(there, X), X)
 
     def relay_copy(there, side):
         place = pl.ds(side * (HALF // 2), HALF // 2)
@@ -165,7 +167,7 @@
 
     def last_copy(there, role):
         side = lax.div(role, 2)
-        half = lax.rem(there, 2)
+        half = lax.div(there, X)
         return remote(
             part.at[there, core],
             last_part.at[half, side],
@@ -195,44 +197,123 @@
             part[there, core, place] = part[there, core, place] + relay[there]
             last_copy(there, role).start()
 
-    def z_step(step):
+    cut = ((0, 48), (48, 32))
+    gz = Ring(Z, z, at_z, lambda b, p: gj.at[b, p], (0, 1), gz_s, gz_r)
+    gy = []
+    for event in range(Z):
+        there = z_of(event)
+        gy.append(
+            Ring(
+                Y,
+                y,
+                at_y,
+                lambda b, p, there=there: gall.at[there, b, core, pl.ds(*cut[p])],
+                (0, 1),
+                gy_s.at[there],
+                gy_r.at[there],
+            )
+        )
+
+    def last_wait(half, side):
+        there = half * X + x
+        remote(
+            part.at[there, core], last_part.at[half, side], lp_s.at[there], lp_r.at[half, side], sibling
+        ).wait_recv()
+
+    def tile_copy(there, d):
+        place = gall.at[there, y, core]
+        return remote(place, place, gt_s.at[there, d - 1], gt_r.at[there], at_x(wrap(x + d, X)))
+
+    def settle(event):
+        there = z_of(event)
+        half = lax.div(there, X)
+
+        @pl.when(role_of(there) == 0)
+        def _():
+            last_wait(half, 0)
+            last_wait(half, 1)
+            tile = (part[there, core] + last_part[half, 0] + last_part[half, 1]).astype(BF16)
+            gj[z, half] = tile
+            gall[there, y, core] = tile
+            for d in (1, 3, 2):
+                tile_copy(there, d).start()
+            gz.send(0, 0, half)
+            gz.send(1, 0, half)
+
+    def share(there, k, core_):
+        place = gall.at[there, wrap(y + k, Y), core_]
+        return remote(place, place, gs_s.at[there, k], gs_r.at[there, k], sibling)
+
+    def spread(event):
+        there = z_of(event)
+
+        @pl.when(role_of(there) != 0)
+        def _():
+            tile_copy(there, 1).wait_recv()
+
+        gy[event].start(0)
+        gy[event].start(1)
+        share(there, 0, core).start()
+
+    def meet(event):
         for way, piece in ((0, 0), (1, 1), (0, 1), (1, 0)):
-            zr.recv(way, step, piece)
-
-    z_step(0)
-    for step in (0, 1):
-        for way, piece in ((0, 0), (1, 1), (0, 1), (1, 0)):
-            yr.recv(way, step, piece)
-    form(0)
-    form(1)
-    form(2)
-    join(0)
-    join(1)
-    join(2)
-    z_step(1)
+            gy[event].recv(way, 0, piece)
+        share(z_of(event), 1, core).start()
+        share(z_of(event), 3, core).start()
+
+    def close(event):
+        gy[event].recv(0, 1, 0)
+        gy[event].recv(1, 1, 1)
+        share(z_of(event), 2, core).start()
+
+    def multiply(event):
+        there = z_of(event)
+        for k in (0, 1, 3, 2):
+            share(there, k, other).wait_recv()
+        square[...] += jnp.dot(
+            gj[there].reshape(ROWS, WIDE), gall[there].reshape(WIDE, WIDE), preferred_element_type=F32
+        )
+
+    def first(ring, step):
+        ring.recv(0, step, 0)
+        ring.recv(1, step, 1)
+
+    def second(ring, step):
+        ring.recv(0, step, 1)
+        ring.recv(1, step, 0)
+
+    def small(refs, slot, send_sems, recv_sems, index, device):
+        return remote(refs.at[slot], refs.at[slot], send_sems.at[index], recv_sems.at[index], device)
+
+    square[...] = jnp.zeros_like(square)
+    first(zr, 0)
+    first(yr, 0)
+    second(zr, 0)
+    second(yr, 0)
+    first(zr, 1)
+    first(yr, 1)
+    for event in (0, 1, 2):
+        form(event)
+    for event in (0, 1, 2):
+        join(event)
+    second(zr, 1)
     form(3)
     form(4)
-    pass_on(0)
-    pass_on(1)
-    pass_on(2)
     join(3)
     join(4)
-    z_step(2)
+    for event in (0, 1, 2):
+        pass_on(event)
+    first(zr, 2)
+    pass_on(3)
+    pass_on(4)
+    second(zr, 2)
     form(5)
     form(6)
-    pass_on(3)
-    pass_on(4)
+    settle(0)
     join(5)
     join(6)
-    z_step(3)
+    first(zr, 3)
     form(7)
-    pass_on(5)
-    pass_on(6)
-    join(7)
-    pass_on(7)
-
-    def small(refs, slot, send_sems, recv_sems, index, device):
-        return remote(refs.at[slot], refs.at[slot], send_sems.at[index], recv_sems.at[index], device)
 
     total = ss_z[0]
     for k in range(1, Z):
@@ -241,36 +322,19 @@
     for d in (1, 2, 3):
         small(ss_y, y, ssy_s, ssy_r, d - 1, at_y(wrap(y + d, Y))).start()
 
-    gz = Ring(Z, z, at_z, lambda b, p: gj.at[b, p], (0, 1), gz_s, gz_r)
-    cut = ((0, 48), (48, 32))
-    gx0 = Ring(X, x, at_x, lambda b, p: gall.at[b, 0, y, core, pl.ds(*cut[p])], (0, 1), gx0_s, gx0_r)
-    gy0 = Ring(Y, y, at_y, lambda b, p: gall.at[wrap(x + p, X), 0, b, core], (0, 0, 1, 1), gy0_s, gy0_r)
-    gy1 = Ring(Y, y, at_y, lambda b, p: gall.at[x, 1, b, core, pl.ds(*cut[p])], (0, 1), gy1_s, gy1_r)
-    gx1 = Ring(X, x, at_x, lambda b, p: gall.at[b, 1, wrap(y + p, Y), core], (0, 0, 1, 1), gx1_s, gx1_r)
-
-    def last_wait(half, side):
-        there = 2 * x + half
-        remote(
-            part.at[there, core], last_part.at[half, side], lp_s.at[there], lp_r.at[half, side], sibling
-        ).wait_recv()
-
-    def settle(half):
-        last_wait(half, 0)
-        last_wait(half, 1)
-        tile = (part[2 * x + half, core] + last_part[half, 0] + last_part[half, 1]).astype(BF16)
-        gj[z, half] = tile
-        gall[x, half, y, core] = tile
-
-    settle(0)
-    gx0.start(0)
-    gx0.start(1)
-    gz.start(0)
-    gy0.start(0)
     settle(1)
-    gy1.start(0)
-    gy1.start(1)
-    gz.start(1)
-    gx1.start(0)
+    settle(2)
+    join(7)
+    settle(3)
+    settle(4)
+    pass_on(5)
+    pass_on(6)
+    spread(0)
+    spread(1)
+    spread(2)
+    pass_on(7)
+    spread(3)
+    spread(4)
 
     for d in (1, 2, 3):
         small(ss_y, wrap(y - d, Y), ssy_s, ssy_r, d - 1, sibling).wait_recv()
@@ -278,98 +342,74 @@
     for d in (1, 2, 3):
         small(ss_x, x, ssx_s, ssx_r, d - 1, at_x(wrap(x + d, X))).start()
 
-    four = ((0, 0), (1, 1), (0, 1), (1, 0))
-
-    def both(ring, step, pieces):
-        for piece in pieces:
-            ring.recv(0, step, piece)
-            ring.recv(1, step, piece)
-
-    def share(half, index, core_):
-        if half == 0:
-            place = gall.at[:, 0, wrap(y + index, Y), core_]
-        else:
-            place = gall.at[wrap(x + index, X), 1, :, core_]
-        return remote(place, place, gs_s.at[half, index], gs_r.at[half, index], sibling)
-
-    for way, piece in four:
-        gx0.recv(way, 0, piece)
-    gy0.start(1)
-    gy0.start(3)
-    for way, piece in four:
-        gy1.recv(way, 0, piece)
-    gx1.start(1)
-    gx1.start(3)
-    both(gz, 0, (0, 1))
-    for way, piece in four:
-        gx0.recv(way, 1, piece)
-    gy0.start(2)
-    for way, piece in four:
-        gy1.recv(way, 1, piece)
-    gx1.start(2)
-    share(0, 0, core).start()
-    share(1, 0, core).start()
+    meet(0)
+    settle(5)
+    settle(6)
+    meet(1)
+    meet(2)
+    settle(7)
+    meet(3)
+    meet(4)
+    spread(5)
+    spread(6)
+    close(0)
+    close(1)
+    close(2)
+    spread(7)
+    close(3)
+    close(4)
+    first(gz, 0)
+    second(gz, 0)
 
     for d in (1, 2, 3):
         small(ss_x, wrap(x - d, X), ssx_s, ssx_r, d - 1, sibling).wait_recv()
     ss_c[core] = ss_x[0] + ss_x[1] + ss_x[2] + ss_x[3]
     small(ss_c, core, ssc_s, ssc_r, 0, sibling).start()
 
-    both(gy0, 0, (0,))
-    both(gx1, 0, (0,))
-    both(gz, 1, (0, 1))
-    both(gy0, 0, (1, 3))
-    both(gx1, 0, (1, 3))
-    both(gz, 2, (0, 1))
-    both(gy0, 0, (2,))
-    both(gx1, 0, (2,))
-    for index in (1, 3):
-        share(0, index, core).start()
-        share(1, index, core).start()
-    both(gz, 3, (0, 1))
-    both(gy0, 1, (0, 1, 2, 3))
-    both(gx1, 1, (0, 1, 2, 3))
-    share(0, 2, core).start()
-    share(1, 2, core).start()
+    meet(5)
+    meet(6)
+    first(gz, 1)
+    second(gz, 1)
+    meet(7)
+    multiply(0)
+    multiply(1)
+    multiply(2)
+    close(5)
+    close(6)
+    first(gz, 2)
+    second(gz, 2)
+    close(7)
+    multiply(3)
+    multiply(4)
     small(ss_c, other, ssc_s, ssc_r, 0, sibling).wait_recv()
     norm_total = (ss_c[0] + ss_c[1])[0:1, 0:1]
     factor = math.sqrt(FULL_ROWS) / (3.0 * (jnp.sqrt(norm_total) + norm_eps))
-    factor_out[...] = jnp.broadcast_to(factor, (8, 128))
-    for index in (0, 1, 3, 2):
-        share(0, index, other).wait_recv()
-        share(1, index, other).wait_recv()
-
-    square[...] = jnp.zeros_like(square)
-
-    @pl.loop(0, Z)
-    def _(there):
-        square[...] += jnp.dot(
-            gj[there].reshape(ROWS, WIDE),
-            gall[lax.div(there, 2), lax.rem(there, 2)].reshape(WIDE, WIDE),
-            preferred_element_type=F32,
-        )
-
-    pr = Ring(X, x, at_x, lambda b, p: pb.at[b, p, core], (0, 1), pr_s, pr_r)
+    factor_out[...] = jnp.broadcast_to(math.sqrt(FULL_COLS) * factor, factor_out.shape)
+    multiply(5)
+    multiply(6)
+    first(gz, 3)
+    multiply(7)
+
+    pr = Ring(X, x, at_x, lambda b, p: pb.at[p, b, core], (0, 1), pr_s, pr_r)
     for half in (0, 1):
         gram = gj[z, half].astype(F32)
         tile = (
             cubic_coef * factor * factor * gram
             + quintic_coef * (factor * factor) * (factor * factor) * square[pl.ds(half * HALF, HALF)]
         )
-        pb[x, half, core] = tile.astype(BF16)
+        pb[half, x, core] = tile.astype(BF16)
         pr.start(half)
 
     def share_p(index, core_):
-        place = pb.at[wrap(x + index, X), :, core_]
+        place = pb.at[:, wrap(x + index, X), core_]
         return remote(place, place, ps_s.at[index], ps_r.at[index], sibling)
 
     share_p(0, core).start()
-    for way, piece in four:
-        pr.recv(way, 0, piece)
+    first(pr, 0)
+    second(pr, 0)
     share_p(1, core).start()
     share_p(3, core).start()
-    for way, piece in four:
-        pr.recv(way, 1, piece)
+    first(pr, 1)
     share_p(2, core).start()
     for index in (0, 1, 3, 2):
         share_p(index, other).wait_recv()
@@ -417,9 +457,12 @@
         for side in (0, 1):
             for half in (0, 1):
                 y_last_copy(tile, side, half).wait_recv()
-        product[:, pl.ds(tile * TILE, TILE)] = up[tile, y] + y_last[tile, 0] + y_last[tile, 1]
-
-    for ring in (zr, yr, gz, gx0, gy0, gy1, gx1, pr):
+        columns = pl.ds(tile * TILE, TILE)
+        product[:, columns] = (
+            linear_coef * xb[z, :, columns].astype(F32) + up[tile, y] + y_last[tile, 0] + y_last[tile, 1]
+        )
+
+    for ring in (zr, yr, gz, pr, *gy):
         ring.finish()
     for event in range(Z):
         there = z_of(event)
@@ -434,14 +477,20 @@
         @pl.when(lax.rem(role, 2) == 1)
         def _():
             last_copy(there, role).wait_send()
+
+        @pl.when(role == 0)
+        def _():
+            for d in (1, 2, 3):
+                tile_copy(there, d).wait_send()
+
+        for k in range(Y):
+            share(there, k, core).wait_send()
 
     for d in (1, 2, 3):
         small(ss_y, y, ssy_s, ssy_r, d - 1, sibling).wait_send()
         small(ss_x, x, ssx_s, ssx_r, d - 1, sibling).wait_send()
     small(ss_c, core, ssc_s, ssc_r, 0, sibling).wait_send()
     for index in range(4):
-        share(0, index, core).wait_send()
-        share(1, index, core).wait_send()
         share_p(index, core).wait_send()
     for tile in range(TILES):
         for side in (0, 1):
@@ -458,15 +507,15 @@
     return [dma(*shape), dma(*shape)]
 
 
-def fused(iterate):
+def fused(momentum, gradient):
     vmem = pl.BlockSpec(memory_space=pltpu.VMEM)
     return pl.pallas_call(
         kernel,
         out_shape=(
             jax.ShapeDtypeStruct((ROWS, COLS), F32),
-            jax.ShapeDtypeStruct((8, 128), F32),
+            jax.ShapeDtypeStruct((1, COLS), F32),
         ),
-        in_specs=[vmem],
+        in_specs=[vmem, vmem],
         out_specs=(vmem, vmem),
         scratch_shapes=[
             pltpu.VMEM((Y, ROWS, COLS), BF16),
@@ -476,8 +525,8 @@
             pltpu.VMEM((Z, HALF // 2, WIDE), F32),
             pltpu.VMEM((2, 2, HALF, WIDE), F32),
             pltpu.VMEM((Z, 2, HALF, WIDE), BF16),
-            pltpu.VMEM((X, 2, Y, 2, HALF, WIDE), BF16),
-            pltpu.VMEM((X, 2, 2, HALF, WIDE), BF16),
+            pltpu.VMEM((Z, Y, 2, HALF, WIDE), BF16),
+            pltpu.VMEM((2, X, 2, HALF, WIDE), BF16),
             pltpu.VMEM((TILES, Y, ROWS, TILE), F32),
             pltpu.VMEM((TILES, 2, HALF, TILE), F32),
             pltpu.VMEM((TILES, 2, ROWS, TILE), F32),
@@ -492,11 +541,9 @@
             dma(Z, 2), dma(Z),
             dma(Z), dma(2, 2),
             *twice(2, 4, 2),
-            *twice(2, 2, 2),
-            *twice(2, 2, 4),
-            *twice(2, 2, 2),
-            *twice(2, 2, 4),
-            *twice(2, 4),
+            dma(Z, 3), dma(Z),
+            *twice(Z, 2, 2, 2),
+            *twice(Z, Y),
             *twice(2, 2, 2),
             *twice(4),
             *twice(3),
@@ -508,14 +555,13 @@
         compiler_params=pltpu.CompilerParams(
             collective_id=0, has_side_effects=True, vmem_limit_bytes=56 * 1024 * 1024
         ),
-    )(iterate)
+    )(momentum, gradient)
 
 
 def local(momentum, gradient):
     new_momentum = decay_rate * momentum + gradient.astype(F32)
-    iterate = new_momentum.astype(BF16)
-    product, factor = fused(iterate)
-    update = math.sqrt(FULL_COLS) * factor[0, 0] * (linear_coef * iterate.astype(F32) + product)
+    product, scale = fused(momentum, gradient)
+    update = scale * product
     return (new_momentum, update)
 
 

time: 139 us -> 132 us (0.950)
  Pallas kernels: 132 us -> 128 us
    pallas_call x1, Pallas kernels: 132 us -> 128 us  [fused(): pl.pallas_call(kernel, out_shape=(jax.ShapeDtypeStruct((ROWS, COLS), F32)...]
    add x0 -> x1, other arithmetic: none -> 2.34 us  [local(): new_momentum = decay_rate * momentum + gradient.astype(F32)]
    convert_element_type x1 -> x0, other arithmetic: 2.3 us -> none  [local(): iterate = new_momentum.astype(BF16)]
    mul x1 -> x0, other arithmetic: 2.08 us -> none  [local(): math.sqrt(FULL_COLS) * factor[0, 0]]
where the time goes in v3:
time: 132 us; the launch traced here: 131 us
  Pallas kernels  128 us (97%)
  other arithmetic  3.05 us (2%)
    pallas_call x1, Pallas kernels, fused(): pl.pallas_call(kernel, out_shape=(jax.ShapeDtypeStruct((ROWS, COLS), F32)...  128 us

profile of v3, /device:TPU:1, one launch (start us, length us, event | category | flops | bytes accessed | tf_op | source)
XLA Modules:
  0.0 131.3 jit_solution(6074921703423405801)
XLA Ops:
  0.6 0.0 copy-start.1
  0.6 0.0 copy-start
  0.6 127.6 %shard_map.41 = (f32[160,1152]{1,0:T(8,128)}, f32[1,1152]{1,0:T(1,128)}) custom-call(f32[160,1152]{1,0:T(8,128)} %momentum.1, bf16[160,1152]{1,0:T(8,128)(2,1)} %gradient.1), custom_call_target="tpu_custom_call" | custom-call | tf_op jit(solution)/shard_map/pallas_call | solution.py:512
  128.3 0.7 reduce
  129.0 0.0 copy-done.1
  129.0 0.0 copy-done
  129.0 2.3 %convert_add_fusion = (f32[160,1152]{1,0:T(8,128)}, f32[160,1152]{1,0:T(8,128)}) fusion(bf16[160,1152]{1,0:T(8,128)(2,1)S(1)} %copy-done.1, f32[160,1152]{1,0:T(8,128)S(1)} %copy-done, f32[160,1152]{1,0:T(8,128)} %get-tuple-element.5, f32[1152]{0:T(1024)S(1)} %reduce), kind=kLoop, calls=%fused_computation | loop fusion | flops 737280 | bytes 3322368 | tf_op jit(solution)/shard_map/add | solution.py:562
Async XLA Ops:
  0.6 128.3 %copy-start.1 = (bf16[160,1152]{1,0:T(8,128)(2,1)S(1)}, bf16[160,1152]{1,0:T(8,128)(2,1)}, u32[]{:S(2)}) copy-start(bf16[160,1152]{1,0:T(8,128)(2,1)} %gradient.1) | copy-start | bytes 1105924
  0.6 128.3 %copy-start = (f32[160,1152]{1,0:T(8,128)S(1)}, f32[160,1152]{1,0:T(8,128)}, u32[]{:S(2)}) copy-start(f32[160,1152]{1,0:T(8,128)} %momentum.1) | copy-start | bytes 2211844

commit v4 on v3

--- a/solution.py
+++ b/solution.py
@@ -17,8 +17,11 @@
 ROWS, COLS = 160, 1152
 HALF = ROWS // 2
 WIDE = Y * ROWS
-TILES = 3
-TILE = COLS // TILES
+UNIT = 16
+EXTRA = pl.ds(UNIT, UNIT)
+TILES = 2
+TILE = COLS // 3
+SPLIT = TILES * TILE
 FULL_ROWS = ROWS * Y * Z
 FULL_COLS = COLS * X * 2
 NT = (((1,), (1,)), ((), ()))
@@ -66,8 +69,8 @@
         sign = 1 - 2 * way
         self.copy(way, step, piece, wrap(self.position - sign * step, self.size)).start()
 
-    def start(self, piece):
-        for way in (0, 1):
+    def start(self):
+        for way, piece in ((0, 0), (1, 1), (0, 1), (1, 0)):
             self.send(way, 0, piece)
 
     def recv(self, way, step, piece):
@@ -94,12 +97,12 @@
     gradient,
     product,
     factor_out,
-    xa, xb, part, sibling_part, relay, last_part, gj, gall, pb, up, y_relay, y_last,
+    xa, xb, part, sibling_part, units, extras, gj, gall, pb, up, y_relay, y_last, uz, z_sum,
     square, ss_z, ss_y, ss_x, ss_c,
-    zr_s, zr_r, yr_s, yr_r, sp_s, sp_r, rl_s, rl_r, lp_s, lp_r,
-    gz_s, gz_r, gt_s, gt_r, gy_s, gy_r, gs_s, gs_r,
+    zr_s, zr_r, yr_s, yr_r, sp_s, sp_r, us_s, us_r, es_s, es_r,
+    gz_s, gz_r, gt_s, gt_r, ge_s, ge_r, gy_s, gy_r, gs_s, gs_r,
     pr_s, pr_r, ps_s, ps_r, ssy_s, ssy_r, ssx_s, ssx_r, ssc_s, ssc_r,
-    ur_s, ur_r, ul_s, ul_r,
+    ur_s, ur_r, ul_s, ul_r, zs_s, zs_r,
 ):
     row, col = lax.axis_index("row"), lax.axis_index("col")
     z, y = lax.div(row, Y), lax.rem(row, Y)
@@ -155,47 +158,39 @@
     def role_of(there):
         return wrap(x - lax.rem(there, X), X)
 
-    def relay_copy(there, side):
-        place = pl.ds(side * (HALF // 2), HALF // 2)
-        return remote(
-            part.at[there, core, place],
-            relay.at[there],
-            rl_s.at[there, side],
-            rl_r.at[there],
-            at_x(wrap(x - 1 + 2 * side, X)),
-        )
-
-    def last_copy(there, role):
-        side = lax.div(role, 2)
-        half = lax.div(there, X)
-        return remote(
-            part.at[there, core],
-            last_part.at[half, side],
-            lp_s.at[there],
-            lp_r.at[half, side],
-            at_x(wrap(x + role - 2, X)),
+    def rows_of(unit):
+        return pl.ds(pl.multiple_of(UNIT * (unit + lax.div(unit + 2, 3)), UNIT), UNIT)
+
+    def unit_copy(there, d):
+        to = wrap(x + d, X)
+        return remote(
+            part.at[there, core, rows_of(wrap(to - lax.rem(there, X), X))],
+            units.at[there, d - 1],
+            us_s.at[there, d - 1],
+            us_r.at[there, d - 1],
+            at_x(to),
+        )
+
+    def extra_copy(there, slot):
+        return remote(
+            part.at[there, core, EXTRA],
+            extras.at[there, slot],
+            es_s.at[there],
+            es_r.at[there, slot],
+            at_x(lax.rem(there, X)),
         )
 
     def join(event):
         there = z_of(event)
         sibling_copy(there).wait_recv()
         part[there, core] = part[there, core] + sibling_part[there]
-
-        @pl.when(role_of(there) == 2)
+        for d in (2, 1, 3):
+            unit_copy(there, d).start()
+        role = role_of(there)
+
+        @pl.when(role != 0)
         def _():
-            relay_copy(there, 0).start()
-            relay_copy(there, 1).start()
-
-    def pass_on(event):
-        there = z_of(event)
-        role = role_of(there)
-
-        @pl.when(lax.rem(role, 2) == 1)
-        def _():
-            relay_copy(there, 0).wait_recv()
-            place = pl.ds(pl.multiple_of(lax.div(role, 2) * (HALF // 2), 8), HALF // 2)
-            part[there, core, place] = part[there, core, place] + relay[there]
-            last_copy(there, role).start()
+            extra_copy(there, 3 - role).start()
 
     cut = ((0, 48), (48, 32))
     gz = Ring(Z, z, at_z, lambda b, p: gj.at[b, p], (0, 1), gz_s, gz_r)
@@ -214,31 +209,37 @@
             )
         )
 
-    def last_wait(half, side):
-        there = half * X + x
-        remote(
-            part.at[there, core], last_part.at[half, side], lp_s.at[there], lp_r.at[half, side], sibling
-        ).wait_recv()
-
     def tile_copy(there, d):
-        place = gall.at[there, y, core]
-        return remote(place, place, gt_s.at[there, d - 1], gt_r.at[there], at_x(wrap(x + d, X)))
+        place = gall.at[there, y, core, rows_of(role_of(there))]
+        return remote(
+            place, place, gt_s.at[there, d - 1], gt_r.at[there, d - 1], at_x(wrap(x + d, X))
+        )
+
+    def extra_tile_copy(there, d):
+        place = gall.at[there, y, core, EXTRA]
+        return remote(place, place, ge_s.at[there, d - 1], ge_r.at[there], at_x(wrap(x + d, X)))
 
     def settle(event):
         there = z_of(event)
-        half = lax.div(there, X)
-
-        @pl.when(role_of(there) == 0)
+        role = role_of(there)
+        rows = rows_of(role)
+        for d in (1, 2, 3):
+            unit_copy(there, d).wait_recv()
+        gall[there, y, core, rows] = (
+            part[there, core, rows] + units[there, 0] + units[there, 1] + units[there, 2]
+        ).astype(BF16)
+        for d in (2, 1, 3):
+            tile_copy(there, d).start()
+
+        @pl.when(role == 0)
         def _():
-            last_wait(half, 0)
-            last_wait(half, 1)
-            tile = (part[there, core] + last_part[half, 0] + last_part[half, 1]).astype(BF16)
-            gj[z, half] = tile
-            gall[there, y, core] = tile
-            for d in (1, 3, 2):
-                tile_copy(there, d).start()
-            gz.send(0, 0, half)
-            gz.send(1, 0, half)
+            for slot in (0, 1, 2):
+                extra_copy(there, slot).wait_recv()
+            gall[there, y, core, EXTRA] = (
+                part[there, core, EXTRA] + extras[there, 0] + extras[there, 1] + extras[there, 2]
+            ).astype(BF16)
+            for d in (2, 1, 3):
+                extra_tile_copy(there, d).start()
 
     def share(there, k, core_):
         place = gall.at[there, wrap(y + k, Y), core_]
@@ -246,14 +247,24 @@
 
     def spread(event):
         there = z_of(event)
-
-        @pl.when(role_of(there) != 0)
+        role = role_of(there)
+        for d in (1, 2, 3):
+            place = gall.at[there, y, core, rows_of(wrap(role - d, X))]
+            remote(place, place, gt_s.at[there, d - 1], gt_r.at[there, d - 1], sibling).wait_recv()
+
+        @pl.when(role != 0)
         def _():
-            tile_copy(there, 1).wait_recv()
-
-        gy[event].start(0)
-        gy[event].start(1)
+            extra_tile_copy(there, 1).wait_recv()
+
+        gy[event].start()
         share(there, 0, core).start()
+
+        @pl.when(role == 0)
+        def _():
+            half = lax.div(there, X)
+            gj[z, half] = gall[there, y, core]
+            gz.send(0, 0, half)
+            gz.send(1, 0, half)
 
     def meet(event):
         for way, piece in ((0, 0), (1, 1), (0, 1), (1, 0)):
@@ -299,21 +310,25 @@
     second(zr, 1)
     form(3)
     form(4)
+    settle(0)
+    first(zr, 2)
+    settle(1)
+    settle(2)
     join(3)
     join(4)
-    for event in (0, 1, 2):
-        pass_on(event)
-    first(zr, 2)
-    pass_on(3)
-    pass_on(4)
     second(zr, 2)
     form(5)
     form(6)
-    settle(0)
+    spread(0)
     join(5)
     join(6)
+    spread(1)
+    spread(2)
     first(zr, 3)
     form(7)
+    settle(3)
+    settle(4)
+    join(7)
 
     total = ss_z[0]
     for k in range(1, Z):
@@ -322,19 +337,14 @@
     for d in (1, 2, 3):
         small(ss_y, y, ssy_s, ssy_r, d - 1, at_y(wrap(y + d, Y))).start()
 
-    settle(1)
-    settle(2)
-    join(7)
-    settle(3)
-    settle(4)
-    pass_on(5)
-    pass_on(6)
-    spread(0)
-    spread(1)
-    spread(2)
-    pass_on(7)
+    meet(0)
     spread(3)
+    meet(1)
     spread(4)
+    settle(5)
+    settle(6)
+    meet(2)
+    close(0)
 
     for d in (1, 2, 3):
         small(ss_y, wrap(y - d, Y), ssy_s, ssy_r, d - 1, sibling).wait_recv()
@@ -342,24 +352,18 @@
     for d in (1, 2, 3):
         small(ss_x, x, ssx_s, ssx_r, d - 1, at_x(wrap(x + d, X))).start()
 
-    meet(0)
-    settle(5)
-    settle(6)
-    meet(1)
-    meet(2)
     settle(7)
-    meet(3)
-    meet(4)
+    close(1)
     spread(5)
     spread(6)
-    close(0)
-    close(1)
+    meet(3)
     close(2)
+    meet(4)
     spread(7)
+    first(gz, 0)
+    second(gz, 0)
     close(3)
     close(4)
-    first(gz, 0)
-    second(gz, 0)
 
     for d in (1, 2, 3):
         small(ss_x, wrap(x - d, X), ssx_s, ssx_r, d - 1, sibling).wait_recv()
@@ -398,7 +402,7 @@
             + quintic_coef * (factor * factor) * (factor * factor) * square[pl.ds(half * HALF, HALF)]
         )
         pb[half, x, core] = tile.astype(BF16)
-        pr.start(half)
+    pr.start()
 
     def share_p(index, core_):
         place = pb.at[:, wrap(x + index, X), core_]
@@ -440,7 +444,37 @@
             up[tile, near, place] = up[tile, near, place] + y_relay[tile, side]
             y_last_copy(tile, side, side).start()
 
-    for tile in range(TILES):
+    def z_sum_copy(way, step, half):
+        sign = 1 - 2 * way
+        return remote(
+            uz.at[wrap(z + sign * (4 - step), Z), pl.ds(half * HALF, HALF)],
+            z_sum.at[way, step, half],
+            zs_s.at[way, step, half],
+            zs_r.at[way, step, half],
+            at_z(wrap(z + sign, Z)),
+        )
+
+    def z_sum_step(step, second_half):
+        for way in (0, 1):
+            half = way if not second_half else 1 - way
+            z_sum_copy(way, step, half).wait_recv()
+            near = wrap(z + (1 - 2 * way) * (3 - step), Z)
+            place = pl.ds(half * HALF, HALF)
+            uz[near, place] = uz[near, place] + z_sum[way, step, half]
+            z_sum_copy(way, step + 1, half).start()
+
+    def begin_z():
+        uz[...] = jnp.dot(
+            pb[...].reshape(Z * ROWS, WIDE),
+            xa[:, :, pl.ds(SPLIT, TILE)].reshape(WIDE, TILE),
+            preferred_element_type=F32,
+        ).reshape(Z, ROWS, TILE)
+        for way in (0, 1):
+            z_sum_copy(way, 0, way).start()
+        for way in (0, 1):
+            z_sum_copy(way, 1, 1 - way).start()
+
+    def begin_y(tile):
         up[tile] = lax.dot_general(
             pb[...].reshape(Z * ROWS, WIDE),
             xb[:, :, pl.ds(tile * TILE, TILE)].reshape(Z * ROWS, TILE),
@@ -449,11 +483,12 @@
         ).reshape(Y, ROWS, TILE)
         for side in (0, 1):
             y_relay_copy(tile, side).start()
+
+    def begin_near(tile):
         for side in (0, 1):
             y_last_copy(tile, side, 1 - side).start()
-    for tile in range(TILES):
-        add_relay(tile)
-    for tile in range(TILES):
+
+    def finish_y(tile):
         for side in (0, 1):
             for half in (0, 1):
                 y_last_copy(tile, side, half).wait_recv()
@@ -462,26 +497,52 @@
             linear_coef * xb[z, :, columns].astype(F32) + up[tile, y] + y_last[tile, 0] + y_last[tile, 1]
         )
 
+    def finish_z(half):
+        for way in (0, 1):
+            z_sum_copy(way, 3, half).wait_recv()
+        rows, columns = pl.ds(half * HALF, HALF), pl.ds(SPLIT, TILE)
+        product[rows, columns] = (
+            linear_coef * xb[z, rows, columns].astype(F32)
+            + uz[z, rows]
+            + z_sum[0, 3, half]
+            + z_sum[1, 3, half]
+        )
+
+    begin_z()
+    begin_y(0)
+    begin_y(1)
+    begin_near(0)
+    begin_near(1)
+    z_sum_step(0, False)
+    add_relay(0)
+    z_sum_step(1, True)
+    add_relay(1)
+    z_sum_step(1, False)
+    z_sum_step(2, True)
+    z_sum_step(2, False)
+    finish_y(0)
+    finish_y(1)
+    finish_z(0)
+    finish_z(1)
+
     for ring in (zr, yr, gz, pr, *gy):
         ring.finish()
     for event in range(Z):
         there = z_of(event)
         sibling_copy(there).wait_send()
         role = role_of(there)
-
-        @pl.when(role == 2)
+        for d in (1, 2, 3):
+            unit_copy(there, d).wait_send()
+            tile_copy(there, d).wait_send()
+
+        @pl.when(role != 0)
         def _():
-            relay_copy(there, 0).wait_send()
-            relay_copy(there, 1).wait_send()
-
-        @pl.when(lax.rem(role, 2) == 1)
-        def _():
-            last_copy(there, role).wait_send()
+            extra_copy(there, 3 - role).wait_send()
 
         @pl.when(role == 0)
         def _():
             for d in (1, 2, 3):
-                tile_copy(there, d).wait_send()
+                extra_tile_copy(there, d).wait_send()
 
         for k in range(Y):
             share(there, k, core).wait_send()
@@ -497,6 +558,11 @@
             y_relay_copy(tile, side).wait_send()
             for half in (0, 1):
                 y_last_copy(tile, side, half).wait_send()
+    for way in (0, 1):
+        z_sum_copy(way, 0, way).wait_send()
+        for step in (1, 2, 3):
+            for half in (0, 1):
+                z_sum_copy(way, step, half).wait_send()
 
 
 def dma(*shape):
@@ -513,7 +579,7 @@
         kernel,
         out_shape=(
             jax.ShapeDtypeStruct((ROWS, COLS), F32),
-            jax.ShapeDtypeStruct((1, COLS), F32),
+            jax.ShapeDtypeStruct((8, COLS), F32),
         ),
         in_specs=[vmem, vmem],
         out_specs=(vmem, vmem),
@@ -522,14 +588,16 @@
             pltpu.VMEM((Z, ROWS, COLS), BF16),
             pltpu.VMEM((Z, 2, HALF, WIDE), F32),
             pltpu.VMEM((Z, HALF, WIDE), F32),
-            pltpu.VMEM((Z, HALF // 2, WIDE), F32),
-            pltpu.VMEM((2, 2, HALF, WIDE), F32),
+            pltpu.VMEM((Z, 3, UNIT, WIDE), F32),
+            pltpu.VMEM((Z, 3, UNIT, WIDE), F32),
             pltpu.VMEM((Z, 2, HALF, WIDE), BF16),
             pltpu.VMEM((Z, Y, 2, HALF, WIDE), BF16),
             pltpu.VMEM((2, X, 2, HALF, WIDE), BF16),
             pltpu.VMEM((TILES, Y, ROWS, TILE), F32),
             pltpu.VMEM((TILES, 2, HALF, TILE), F32),
             pltpu.VMEM((TILES, 2, ROWS, TILE), F32),
+            pltpu.VMEM((Z, ROWS, TILE), F32),
+            pltpu.VMEM((2, 4, 2, HALF, TILE), F32),
             pltpu.VMEM((ROWS, WIDE), F32),
             pltpu.VMEM((Z, 8, 128), F32),
             pltpu.VMEM((Y, 8, 128), F32),
@@ -538,9 +606,10 @@
             *twice(2, 4, 2),
             *twice(2, 2, 2),
             *twice(Z),
-            dma(Z, 2), dma(Z),
-            dma(Z), dma(2, 2),
+            *twice(Z, 3),
+            dma(Z), dma(Z, 3),
             *twice(2, 4, 2),
+            *twice(Z, 3),
             dma(Z, 3), dma(Z),
             *twice(Z, 2, 2, 2),
             *twice(Z, Y),
@@ -551,6 +620,7 @@
             *twice(1),
             *twice(TILES, 2),
             *twice(TILES, 2, 2),
+            *twice(2, 4, 2),
         ],
         compiler_params=pltpu.CompilerParams(
             collective_id=0, has_side_effects=True, vmem_limit_bytes=56 * 1024 * 1024
@@ -561,7 +631,7 @@
 def local(momentum, gradient):
     new_momentum = decay_rate * momentum + gradient.astype(F32)
     product, scale = fused(momentum, gradient)
-    update = scale * product
+    update = (scale * product.reshape(ROWS // 8, 8, COLS)).reshape(ROWS, COLS)
     return (new_momentum, update)
 
 

time: 132 us -> 119 us (0.902)
  Pallas kernels: 128 us -> 116 us
    pallas_call x1, Pallas kernels: 128 us -> 116 us  [fused(): pl.pallas_call(kernel, out_shape=(jax.ShapeDtypeStruct((ROWS, COLS), F32)...]
    add x1 -> x0, other arithmetic: 2.34 us -> none  [local(): new_momentum = decay_rate * momentum + gradient.astype(F32)]
    mul x0 -> x1, other arithmetic: none -> 2.34 us  [local(): update = (scale * product.reshape(ROWS // 8, 8, COLS)).reshape(ROWS, COLS)]
where the time goes in v4:
time: 119 us
  Pallas kernels  116 us (97%)
  other arithmetic  2.34 us (2%)
    pallas_call x1, Pallas kernels, fused(): pl.pallas_call(kernel, out_shape=(jax.ShapeDtypeStruct((ROWS, COLS), F32)...  116 us

profile of v4, /device:TPU:1, one launch (start us, length us, event | category | flops | bytes accessed | tf_op | source)
XLA Modules:
  0.0 119.3 jit_solution(16641247177555469194)
XLA Ops:
  0.6 0.0 copy-start.1
  0.6 0.0 copy-start
  0.6 116.2 %shard_map.41 = (f32[160,1152]{1,0:T(8,128)}, f32[8,1152]{1,0:T(8,128)}) custom-call(f32[160,1152]{1,0:T(8,128)} %momentum.1, bf16[160,1152]{1,0:T(8,128)(2,1)} %gradient.1), custom_call_target="tpu_custom_call" | custom-call | tf_op jit(solution)/shard_map/pallas_call | solution.py:578
  116.9 0.0 copy-done.1
  116.9 0.0 copy-done
  116.9 2.3 %bitcast_multiply_fusion = (f32[160,1152]{1,0:T(8,128)}, f32[160,1152]{1,0:T(8,128)}) fusion(f32[160,1152]{1,0:T(8,128)} %get-tuple-element.5, f32[8,1152]{1,0:T(8,128)} %get-tuple-element.4, bf16[160,1152]{1,0:T(8,128)(2,1)S(1)} %copy-done.1, f32[160,1152]{1,0:T(8,128)S(1)} %copy-done), kind=kLoop, calls=%fused_computation | loop fusion | flops 737280 | bytes 3354624 | tf_op jit(solution)/shard_map/mul | solution.py:634
Async XLA Ops:
  0.6 116.3 %copy-start.1 = (bf16[160,1152]{1,0:T(8,128)(2,1)S(1)}, bf16[160,1152]{1,0:T(8,128)(2,1)}, u32[]{:S(2)}) copy-start(bf16[160,1152]{1,0:T(8,128)(2,1)} %gradient.1) | copy-start | bytes 1105924
  0.6 116.3 %copy-start = (f32[160,1152]{1,0:T(8,128)S(1)}, f32[160,1152]{1,0:T(8,128)}, u32[]{:S(2)}) copy-start(f32[160,1152]{1,0:T(8,128)} %momentum.1) | copy-start | bytes 2211844

commit v5 on v4

v5 whole, which is shorter than its diff:
```python
import math

import jax
import jax.numpy as jnp
from jax import lax
from jax.experimental import pallas as pl
from jax.experimental.pallas import tpu as pltpu
from jax.sharding import PartitionSpec as P

decay_rate = 0.95
linear_coef = 3.4445
cubic_coef = -4.775
quintic_coef = 2.0315
norm_eps = 1e-07

X, Y, Z = 4, 4, 8
ROWS, COLS = 160, 1152
HALF = ROWS // 2
WIDE = Y * ROWS
UNIT = 16
EXTRA = pl.ds(UNIT, UNIT)
TILES = 2
TILE = COLS // 3
SPLIT = TILES * TILE
FULL_ROWS = ROWS * Y * Z
FULL_COLS = COLS * X * 2
NT = (((1,), (1,)), ((), ()))
TN = (((0,), (0,)), ((), ()))
F32 = jnp.float32
BF16 = jnp.bfloat16


def wrap(value, size):
    return lax.rem(value + size, size)


def remote(src, dst, send_sem, recv_sem, device):
    return pltpu.make_async_remote_copy(
        src_ref=src,
        dst_ref=dst,
        send_sem=send_sem,
        recv_sem=recv_sem,
        device_id=device,
        device_id_type=pl.DeviceIdType.MESH,
    )


class Ring:
    def __init__(self, size, position, device, region, last, send_sem, recv_sems):
        self.size, self.position, self.device = size, position, device
        self.region, self.last = region, last
        self.send_sem, self.recv_sems = send_sem, recv_sems
        self.slots = {}
        for way in (0, 1):
            for piece in range(len(last)):
                for step in range(size // 2 - (0 if last[piece] == way else 1)):
                    self.slots[way, step, piece] = len(self.slots)

    def copy(self, way, step, piece, block):
        sign = 1 - 2 * way
        place = self.region(block, piece)
        return remote(
            place,
            place,
            self.send_sem,
            self.recv_sems.at[self.slots[way, step, piece]],
            self.device(wrap(self.position + sign, self.size)),
        )

    def send(self, way, step, piece):
        sign = 1 - 2 * way
        self.copy(way, step, piece, wrap(self.position - sign * step, self.size)).start()

    def start(self):
        for way, piece in ((0, 0), (1, 1), (0, 1), (1, 0)):
            self.send(way, 0, piece)

    def recv(self, way, step, piece):
        if (way, step, piece) not in self.slots:
            return
        sign = 1 - 2 * way
        self.copy(way, step, piece, wrap(self.position - sign * (step + 1), self.size)).wait_recv()
        if (way, step + 1, piece) in self.slots:
            self.send(way, step + 1, piece)


OFFSETS = (0, 1, -1, 2, -2, 3, -3, 4)


def kernel(
    momentum,
    gradient,
    product,
    factor_out,
    xa, xb, part, sibling_part, units, gj, gall, pb, up, y_relay, y_last, uz, z_sum,
    square, ss_z, ss_y, ss_x, ss_c,
    sent, zr_r, yr_r, sp_r, us_r, gz_r, gt_r, gy_r, gs_r, pr_r, ps_r, ss_r, ur_r, ul_r, zs_r,
):
    row, col = lax.axis_index("row"), lax.axis_index("col")
    z, y = lax.div(row, Y), lax.rem(row, Y)
    x, core = lax.div(col, 2), lax.rem(col, 2)
    other = 1 - core

    def at_z(p):
        return (p * Y + y, col)

    def at_y(p):
        return (z * Y + p, col)

    def at_x(p):
        return (row, p * 2 + core)

    sibling = (row, x * 2 + other)

    barrier = pltpu.get_barrier_semaphore()
    partners = [at_z(wrap(z + d, Z)) for d in (1, -1, 2, -2)] + [sibling]
    partners += [at_y(wrap(y + d, Y)) for d in (1, 2, 3)]
    partners += [at_x(wrap(x + d, X)) for d in (1, 2, 3)]
    for partner in partners:
        pl.semaphore_signal(barrier, inc=1, device_id=partner, device_id_type=pl.DeviceIdType.MESH)
    iterate = (decay_rate * momentum[...] + gradient[...].astype(F32)).astype(BF16)
    xb[z] = iterate
    xa[y] = iterate
    pl.semaphore_wait(barrier, len(partners))

    zr = Ring(Z, z, at_z, lambda b, p: xb.at[b, pl.ds(p * HALF, HALF)], (0, 1), sent.at[0], zr_r)
    yr = Ring(Y, y, at_y, lambda b, p: xa.at[b, pl.ds(p * HALF, HALF)], (0, 1), sent.at[1], yr_r)
    for way, piece in ((0, 0), (1, 1), (0, 1), (1, 0)):
        zr.send(way, 0, piece)
        yr.send(way, 0, piece)

    def z_of(event):
        return wrap(z + OFFSETS[event], Z)

    def sibling_copy(there):
        return remote(
            part.at[there, other], sibling_part.at[there], sent.at[2], sp_r.at[there], sibling
        )

    def form(event):
        there = z_of(event)
        block = xb[there]
        part[there] = lax.dot_general(
            block, xa[...].reshape(WIDE, COLS), NT, preferred_element_type=F32
        ).reshape(2, HALF, WIDE)
        sibling_copy(there).start()
        wide = block.astype(F32)
        ss_z[there] = jnp.broadcast_to(jnp.sum(wide * wide, keepdims=True), (8, 128))

    def role_of(there):
        return wrap(x - lax.rem(there, X), X)

    def rows_of(unit):
        return pl.ds(pl.multiple_of(UNIT * (unit + lax.div(unit + 2, 3)), UNIT), UNIT)

    def unit_copy(there, d):
        to = wrap(x + d, X)
        return remote(
            part.at[there, core, rows_of(wrap(to - lax.rem(there, X), X))],
            units.at[there, d - 1],
            sent.at[3],
            us_r.at[there],
            at_x(to),
        )

    def extra_copy(there, slot):
        return remote(
            part.at[there, core, EXTRA],
            units.at[there, 3 + slot],
            sent.at[3],
            us_r.at[there],
            at_x(lax.rem(there, X)),
        )

    def join(event):
        there = z_of(event)
        sibling_copy(there).wait_recv()
        part[there, core] = part[there, core] + sibling_part[there]
        for d in (2, 1, 3):
            unit_copy(there, d).start()
        role = role_of(there)

        @pl.when(role != 0)
        def _():
            extra_copy(there, 3 - role).start()

    cut = ((0, 48), (48, 32))
    def panel_copy(way, hops, block, slot, piece):
        place = gj.at[block, piece]
        return remote(
            place, place, sent.at[4], gz_r.at[slot], at_z(wrap(z + (1 - 2 * way) * hops, Z))
        )

    def panel_start(piece):
        for hops in (2, 1):
            for way in (0, 1):
                panel_copy(way, hops, z, 4 * (hops - 1) + 2 * way + piece, piece).start()

    def panel_wait(distance):
        for way in (0, 1):
            for piece in (0, 1) if distance < 4 else (way,):
                slot = 4 * (distance - 1) + (2 * way + piece if distance < 4 else way)
                block = wrap(z - (1 - 2 * way) * distance, Z)
                panel_copy(way, 1, block, slot, piece).wait_recv()
                if distance == 2:
                    if piece == way:
                        panel_copy(way, 2, block, 12 + way, piece).start()
                    panel_copy(way, 1, block, 8 + 2 * way + piece, piece).start()

    gy = []
    for event in range(Z):
        there = z_of(event)
        gy.append(
            Ring(
                Y,
                y,
                at_y,
                lambda b, p, there=there: gall.at[there, b, core, pl.ds(*cut[p])],
                (0, 1),
                sent.at[6],
                gy_r.at[there],
            )
        )

    def tile_copy(there, d):
        place = gall.at[there, y, core, rows_of(role_of(there))]
        return remote(place, place, sent.at[5], gt_r.at[there], at_x(wrap(x + d, X)))

    def extra_tile_copy(there, d):
        place = gall.at[there, y, core, EXTRA]
        return remote(place, place, sent.at[5], gt_r.at[there], at_x(wrap(x + d, X)))

    def landed(place, sem):
        remote(place, place, sent.at[0], sem, sibling).wait_recv()

    def settle(event):
        there = z_of(event)
        role = role_of(there)
        rows = rows_of(role)

        @pl.when(role == 0)
        def _():
            landed(units.at[there], us_r.at[there])
            gall[there, y, core, EXTRA] = (
                part[there, core, EXTRA] + units[there, 3] + units[there, 4] + units[there, 5]
            ).astype(BF16)
            for d in (2, 1, 3):
                extra_tile_copy(there, d).start()

        @pl.when(role != 0)
        def _():
            landed(units.at[there, pl.ds(0, 3)], us_r.at[there])

        gall[there, y, core, rows] = (
            part[there, core, rows] + units[there, 0] + units[there, 1] + units[there, 2]
        ).astype(BF16)
        for d in (2, 1, 3):
            tile_copy(there, d).start()

    def share(there, k, core_):
        place = gall.at[there, wrap(y + k, Y), core_]
        return remote(place, place, sent.at[7], gs_r.at[there], sibling)

    def spread(event):
        there = z_of(event)
        role = role_of(there)
        @pl.when(role == 0)
        def _():
            landed(gall.at[there, y, core, pl.ds(0, 3 * UNIT)], gt_r.at[there])

        @pl.when(role != 0)
        def _():
            landed(gall.at[there, y, core, pl.ds(0, 4 * UNIT)], gt_r.at[there])

        gy[event].start()
        share(there, 0, core).start()

        @pl.when(role == 0)
        def _():
            half = lax.div(there, X)
            gj[z, half] = gall[there, y, core]
            panel_start(half)

    def meet(event):
        for way, piece in ((0, 0), (1, 1), (0, 1), (1, 0)):
            gy[event].recv(way, 0, piece)
        share(z_of(event), 1, core).start()
        share(z_of(event), 3, core).start()

    def close(event):
        gy[event].recv(0, 1, 0)
        gy[event].recv(1, 1, 1)
        share(z_of(event), 2, core).start()

    def multiply(event):
        there = z_of(event)
        landed(gall.at[there, :, other], gs_r.at[there])
        square[...] += jnp.dot(
            gj[there].reshape(ROWS, WIDE), gall[there].reshape(WIDE, WIDE), preferred_element_type=F32
        )

    def first(ring, step):
        ring.recv(0, step, 0)
        ring.recv(1, step, 1)

    def second(ring, step):
        ring.recv(0, step, 1)
        ring.recv(1, step, 0)

    def small(refs, slot, index, device):
        return remote(refs.at[slot], refs.at[slot], sent.at[10 + index], ss_r.at[index], device)

    square[...] = jnp.zeros_like(square)
    first(zr, 0)
    first(yr, 0)
    second(zr, 0)
    second(yr, 0)
    first(zr, 1)
    first(yr, 1)
    for event in (0, 1, 2):
        form(event)
    for event in (0, 1, 2):
        join(event)
    second(zr, 1)
    form(3)
    form(4)
    settle(0)
    first(zr, 2)
    settle(1)
    settle(2)
    join(3)
    join(4)
    second(zr, 2)
    form(5)
    form(6)
    spread(0)
    spread(1)
    spread(2)
    first(zr, 3)
    form(7)
    settle(3)
    join(5)
    settle(4)
    join(6)
    join(7)

    total = ss_z[0]
    for k in range(1, Z):
        total = total + ss_z[k]
    ss_y[y] = total
    for d in (1, 2, 3):
        small(ss_y, y, 0, at_y(wrap(y + d, Y))).start()

    meet(0)
    meet(1)
    spread(3)
    spread(4)
    meet(2)
    close(0)
    settle(5)
    settle(6)
    close(1)
    settle(7)

    landed(ss_y.at[pl.ds(0, 3)], ss_r.at[0])
    ss_x[x] = ss_y[0] + ss_y[1] + ss_y[2] + ss_y[3]
    for d in (1, 2, 3):
        small(ss_x, x, 1, at_x(wrap(x + d, X))).start()

    meet(3)
    close(2)
    spread(5)
    spread(6)
    meet(4)
    spread(7)
    close(3)
    close(4)

    landed(ss_x.at[pl.ds(0, 3)], ss_r.at[1])
    ss_c[core] = ss_x[0] + ss_x[1] + ss_x[2] + ss_x[3]
    small(ss_c, core, 2, sibling).start()

    meet(5)
    panel_wait(2)
    meet(6)
    meet(7)
    multiply(0)
    close(5)
    close(6)
    panel_wait(1)
    multiply(1)
    multiply(2)
    close(7)
    multiply(3)
    multiply(4)
    small(ss_c, other, 2, sibling).wait_recv()
    norm_total = (ss_c[0] + ss_c[1])[0:1, 0:1]
    factor = math.sqrt(FULL_ROWS) / (3.0 * (jnp.sqrt(norm_total) + norm_eps))
    factor_out[...] = jnp.broadcast_to(math.sqrt(FULL_COLS) * factor, factor_out.shape)
    panel_wait(3)
    multiply(5)
    multiply(6)
    panel_wait(4)
    multiply(7)

    pr = Ring(X, x, at_x, lambda b, p: pb.at[p, b, core], (0, 1), sent.at[8], pr_r)
    for half in (0, 1):
        gram = gj[z, half].astype(F32)
        tile = (
            cubic_coef * factor * factor * gram
            + quintic_coef * (factor * factor) * (factor * factor) * square[pl.ds(half * HALF, HALF)]
        )
        pb[half, x, core] = tile.astype(BF16)
    pr.start()

    def share_p(index, core_):
        place = pb.at[:, wrap(x + index, X), core_]
        return remote(place, place, sent.at[9], ps_r.at[index], sibling)

    def y_relay_copy(tile, side):
        return remote(
            up.at[tile, wrap(y + 2, Y), pl.ds(side * HALF, HALF)],
            y_relay.at[tile, side],
            sent.at[13],
            ur_r.at[tile, side],
            at_y(wrap(y + 1 - 2 * side, Y)),
        )

    def y_last_copy(tile, side, half):
        return remote(
            up.at[tile, wrap(y + 1 - 2 * side, Y), pl.ds(half * HALF, HALF)],
            y_last.at[tile, side, pl.ds(half * HALF, HALF)],
            sent.at[14],
            ul_r.at[tile, side, half],
            at_y(wrap(y + 1 - 2 * side, Y)),
        )

    def add_relay(tile):
        for side in (0, 1):
            y_relay_copy(tile, side).wait_recv()
            near = wrap(y + 1 - 2 * side, Y)
            place = pl.ds(side * HALF, HALF)
            up[tile, near, place] = up[tile, near, place] + y_relay[tile, side]
            y_last_copy(tile, side, side).start()

    def z_sum_copy(way, step, half):
        sign = 1 - 2 * way
        return remote(
            uz.at[wrap(z + sign * (4 - step), Z), pl.ds(half * HALF, HALF)],
            z_sum.at[way, step, half],
            sent.at[15],
            zs_r.at[way, step, half],
            at_z(wrap(z + sign, Z)),
        )

    def z_sum_step(step, second_half):
        for way in (0, 1):
            half = way if not second_half else 1 - way
            z_sum_copy(way, step, half).wait_recv()
            near = wrap(z + (1 - 2 * way) * (3 - step), Z)
            place = pl.ds(half * HALF, HALF)
            uz[near, place] = uz[near, place] + z_sum[way, step, half]
            z_sum_copy(way, step + 1, half).start()

    def grow(index):
        there = wrap(x + index, X)
        landed(pb.at[:, there, other], ps_r.at[index])
        for half in (0, 1):
            uz[there + half * X] = jnp.dot(
                pb[half, there].reshape(ROWS, WIDE),
                xa[:, :, pl.ds(SPLIT, TILE)].reshape(WIDE, TILE),
                preferred_element_type=F32,
            )
        if index == 2:
            for way in (0, 1):
                z_sum_copy(way, 0, way).start()
            for way in (0, 1):
                z_sum_copy(way, 1, 1 - way).start()
        for tile in range(TILES):
            columns = pl.ds(tile * TILE, TILE)
            term = lax.dot_general(
                pb[:, there].reshape(2 * ROWS, WIDE),
                jnp.concatenate([xb[there, :, columns], xb[there + X, :, columns]], axis=0),
                TN,
                preferred_element_type=F32,
            ).reshape(Y, ROWS, TILE)
            up[tile] = term if index == 0 else up[tile] + term
            if index == 2:
                for side in (0, 1):
                    y_relay_copy(tile, side).start()

    def begin_near(tile):
        for side in (0, 1):
            y_last_copy(tile, side, 1 - side).start()

    def finish_y(tile):
        for side in (0, 1):
            for half in (0, 1):
                y_last_copy(tile, side, half).wait_recv()
        columns = pl.ds(tile * TILE, TILE)
        product[:, columns] = (
            linear_coef * xb[z, :, columns].astype(F32) + up[tile, y] + y_last[tile, 0] + y_last[tile, 1]
        )

    def finish_z(half):
        for way in (0, 1):
            z_sum_copy(way, 3, half).wait_recv()
        rows, columns = pl.ds(half * HALF, HALF), pl.ds(SPLIT, TILE)
        product[rows, columns] = (
            linear_coef * xb[z, rows, columns].astype(F32)
            + uz[z, rows]
            + z_sum[0, 3, half]
            + z_sum[1, 3, half]
        )

    share_p(0, core).start()
    grow(0)
    first(pr, 0)
    second(pr, 0)
    share_p(1, core).start()
    share_p(3, core).start()
    grow(1)
    first(pr, 1)
    share_p(2, core).start()
    grow(3)
    grow(2)
    begin_near(0)
    begin_near(1)
    z_sum_step(0, False)
    add_relay(0)
    z_sum_step(1, True)
    add_relay(1)
    z_sum_step(1, False)
    z_sum_step(2, True)
    z_sum_step(2, False)
    finish_y(0)
    finish_y(1)
    finish_z(0)
    finish_z(1)

    for index, place in enumerate((
        xb.at[pl.ds(0, 7)],
        xa.at[pl.ds(0, 3)],
        part.at[:, 0],
        units.at[pl.ds(0, 5)],
        gj.at[pl.ds(0, 7)],
        gall.at[pl.ds(0, 3), pl.ds(0, 2), 0],
        gall.at[:, pl.ds(0, 3), 0],
        gall.at[:, :, 0],
        pb.at[0, pl.ds(0, 3)],
        pb.at[:, :, 0],
        ss_y.at[pl.ds(0, 3)],
        ss_x.at[pl.ds(0, 3)],
        ss_c.at[0],
        y_relay,
        y_last,
        uz.at[pl.ds(0, 7)],
    )):
        remote(place, place, sent.at[index], zr_r.at[0], sibling).wait_send()


def dma(*shape):
    return pltpu.SemaphoreType.DMA(shape)


def fused(momentum, gradient):
    vmem = pl.BlockSpec(memory_space=pltpu.VMEM)
    return pl.pallas_call(
        kernel,
        out_shape=(
            jax.ShapeDtypeStruct((ROWS, COLS), F32),
            jax.ShapeDtypeStruct((8, COLS), F32),
        ),
        in_specs=[vmem, vmem],
        out_specs=(vmem, vmem),
        scratch_shapes=[
            pltpu.VMEM((Y, ROWS, COLS), BF16),
            pltpu.VMEM((Z, ROWS, COLS), BF16),
            pltpu.VMEM((Z, 2, HALF, WIDE), F32),
            pltpu.VMEM((Z, HALF, WIDE), F32),
            pltpu.VMEM((Z, 6, UNIT, WIDE), F32),
            pltpu.VMEM((Z, 2, HALF, WIDE), BF16),
            pltpu.VMEM((Z, Y, 2, HALF, WIDE), BF16),
            pltpu.VMEM((2, X, 2, HALF, WIDE), BF16),
            pltpu.VMEM((TILES, Y, ROWS, TILE), F32),
            pltpu.VMEM((TILES, 2, HALF, TILE), F32),
            pltpu.VMEM((TILES, 2, ROWS, TILE), F32),
            pltpu.VMEM((Z, ROWS, TILE), F32),
            pltpu.VMEM((2, 4, 2, HALF, TILE), F32),
            pltpu.VMEM((ROWS, WIDE), F32),
            pltpu.VMEM((Z, 8, 128), F32),
            pltpu.VMEM((Y, 8, 128), F32),
            pltpu.VMEM((X, 8, 128), F32),
            pltpu.VMEM((2, 8, 128), F32),
            dma(16),
            dma(14),
            dma(6),
            dma(Z),
            dma(Z),
            dma(14),
            dma(Z),
            dma(Z, 6),
            dma(Z),
            dma(6),
            dma(X),
            dma(3),
            dma(TILES, 2),
            dma(TILES, 2, 2),
            dma(2, 4, 2),
        ],
        compiler_params=pltpu.CompilerParams(
            collective_id=0, has_side_effects=True, vmem_limit_bytes=56 * 1024 * 1024
        ),
    )(momentum, gradient)


def local(momentum, gradient):
    new_momentum = decay_rate * momentum + gradient.astype(F32)
    product, scale = fused(momentum, gradient)
    update = (scale * product.reshape(ROWS // 8, 8, COLS)).reshape(ROWS, COLS)
    return (new_momentum, update)


def solution(mesh):
    placed = (P("row", "col"), P("row", "col"))
    return jax.shard_map(
        local,
        mesh=mesh,
        in_specs=placed,
        out_specs=(P("row", "col"), P("row", "col")),
        check_vma=False,
    )
```

time: 119 us -> 115 us (0.966)
  Pallas kernels: 116 us -> 112 us
    pallas_call x1, Pallas kernels: 116 us -> 112 us  [fused(): pl.pallas_call(kernel, out_shape=(jax.ShapeDtypeStruct((ROWS, COLS), F32)...]
where the time goes in v5:
time: 115 us
  Pallas kernels  112 us (97%)
  other arithmetic  2.34 us (2%)
    pallas_call x1, Pallas kernels, fused(): pl.pallas_call(kernel, out_shape=(jax.ShapeDtypeStruct((ROWS, COLS), F32)...  112 us
    mul x1, other arithmetic, local(): update = (scale * product.reshape(ROWS // 8, 8, COLS)).reshape(ROWS, COLS)  2.34 us

profile of v5, /device:TPU:1, one launch (start us, length us, event | category | flops | bytes accessed | tf_op | source)
XLA Modules:
  0.0 115.2 jit_solution(12429401445065255462)
XLA Ops:
  0.6 0.0 copy-start.1
  0.6 0.0 copy-start
  0.6 112.2 %shard_map.41 = (f32[160,1152]{1,0:T(8,128)}, f32[8,1152]{1,0:T(8,128)}) custom-call(f32[160,1152]{1,0:T(8,128)} %momentum.1, bf16[160,1152]{1,0:T(8,128)(2,1)} %gradient.1), custom_call_target="tpu_custom_call" | custom-call | tf_op jit(solution)/shard_map/pallas_call | solution.py:568
  112.8 0.0 copy-done.1
  112.8 0.0 copy-done
  112.8 2.3 %bitcast_multiply_fusion = (f32[160,1152]{1,0:T(8,128)}, f32[160,1152]{1,0:T(8,128)}) fusion(f32[160,1152]{1,0:T(8,128)} %get-tuple-element.5, f32[8,1152]{1,0:T(8,128)} %get-tuple-element.4, bf16[160,1152]{1,0:T(8,128)(2,1)S(1)} %copy-done.1, f32[160,1152]{1,0:T(8,128)S(1)} %copy-done), kind=kLoop, calls=%fused_computation | loop fusion | flops 737280 | bytes 3354624 | tf_op jit(solution)/shard_map/mul | solution.py:620
Async XLA Ops:
  0.6 112.2 %copy-start.1 = (bf16[160,1152]{1,0:T(8,128)(2,1)S(1)}, bf16[160,1152]{1,0:T(8,128)(2,1)}, u32[]{:S(2)}) copy-start(bf16[160,1152]{1,0:T(8,128)(2,1)} %gradient.1) | copy-start | bytes 1105924
  0.6 112.2 %copy-start = (f32[160,1152]{1,0:T(8,128)S(1)}, f32[160,1152]{1,0:T(8,128)}, u32[]{:S(2)}) copy-start(f32[160,1152]{1,0:T(8,128)} %momentum.1) | copy-start | bytes 2211844

commit v6 on v5

--- a/solution.py
+++ b/solution.py
@@ -317,28 +317,30 @@
     second(yr, 0)
     first(zr, 1)
     first(yr, 1)
-    for event in (0, 1, 2):
-        form(event)
-    for event in (0, 1, 2):
-        join(event)
+    form(0)
+    form(1)
+    join(0)
+    form(2)
+    join(1)
+    join(2)
     second(zr, 1)
     form(3)
     form(4)
     settle(0)
+    join(3)
     first(zr, 2)
     settle(1)
     settle(2)
-    join(3)
     join(4)
     second(zr, 2)
     form(5)
     form(6)
     spread(0)
     spread(1)
+    settle(3)
     spread(2)
     first(zr, 3)
     form(7)
-    settle(3)
     join(5)
     settle(4)
     join(6)
@@ -352,46 +354,46 @@
         small(ss_y, y, 0, at_y(wrap(y + d, Y))).start()
 
     meet(0)
+    spread(3)
     meet(1)
-    spread(3)
+    settle(5)
     spread(4)
     meet(2)
     close(0)
-    settle(5)
     settle(6)
     close(1)
     settle(7)
+    meet(3)
 
     landed(ss_y.at[pl.ds(0, 3)], ss_r.at[0])
     ss_x[x] = ss_y[0] + ss_y[1] + ss_y[2] + ss_y[3]
     for d in (1, 2, 3):
         small(ss_x, x, 1, at_x(wrap(x + d, X))).start()
 
-    meet(3)
+    spread(5)
     close(2)
-    spread(5)
+    meet(4)
     spread(6)
-    meet(4)
     spread(7)
     close(3)
-    close(4)
 
     landed(ss_x.at[pl.ds(0, 3)], ss_r.at[1])
     ss_c[core] = ss_x[0] + ss_x[1] + ss_x[2] + ss_x[3]
     small(ss_c, core, 2, sibling).start()
 
+    close(4)
     meet(5)
     panel_wait(2)
     meet(6)
     meet(7)
     multiply(0)
-    close(5)
-    close(6)
     panel_wait(1)
     multiply(1)
     multiply(2)
+    close(5)
+    close(6)
+    multiply(3)
     close(7)
-    multiply(3)
     multiply(4)
     small(ss_c, other, 2, sibling).wait_recv()
     norm_total = (ss_c[0] + ss_c[1])[0:1, 0:1]

time: 115 us -> 112 us (0.974)
  Pallas kernels: 112 us -> 109 us
    pallas_call x1, Pallas kernels: 112 us -> 109 us  [fused(): pl.pallas_call(kernel, out_shape=(jax.ShapeDtypeStruct((ROWS, COLS), F32)...]
where the time goes in v6:
time: 112 us
  Pallas kernels  109 us (97%)
  other arithmetic  2.34 us (2%)
    pallas_call x1, Pallas kernels, fused(): pl.pallas_call(kernel, out_shape=(jax.ShapeDtypeStruct((ROWS, COLS), F32)...  109 us
    mul x1, other arithmetic, local(): update = (scale * product.reshape(ROWS // 8, 8, COLS)).reshape(ROWS, COLS)  2.34 us

profile of v6, /device:TPU:1, one launch (start us, length us, event | category | flops | bytes accessed | tf_op | source)
XLA Modules:
  0.0 111.9 jit_solution(12295590341883717003)
XLA Ops:
  0.6 0.0 copy-start.1
  0.6 0.0 copy-start
  0.6 108.9 %shard_map.41 = (f32[160,1152]{1,0:T(8,128)}, f32[8,1152]{1,0:T(8,128)}) custom-call(f32[160,1152]{1,0:T(8,128)} %momentum.1, bf16[160,1152]{1,0:T(8,128)(2,1)} %gradient.1), custom_call_target="tpu_custom_call" | custom-call | tf_op jit(solution)/shard_map/pallas_call | solution.py:570
  109.6 0.0 copy-done.1
  109.6 0.0 copy-done
  109.6 2.3 %bitcast_multiply_fusion = (f32[160,1152]{1,0:T(8,128)}, f32[160,1152]{1,0:T(8,128)}) fusion(f32[160,1152]{1,0:T(8,128)} %get-tuple-element.5, f32[8,1152]{1,0:T(8,128)} %get-tuple-element.4, bf16[160,1152]{1,0:T(8,128)(2,1)S(1)} %copy-done.1, f32[160,1152]{1,0:T(8,128)S(1)} %copy-done), kind=kLoop, calls=%fused_computation | loop fusion | flops 737280 | bytes 3354624 | tf_op jit(solution)/shard_map/mul | solution.py:622
Async XLA Ops:
  0.6 108.9 %copy-start.1 = (bf16[160,1152]{1,0:T(8,128)(2,1)S(1)}, bf16[160,1152]{1,0:T(8,128)(2,1)}, u32[]{:S(2)}) copy-start(bf16[160,1152]{1,0:T(8,128)(2,1)} %gradient.1) | copy-start | bytes 1105924
  0.6 108.9 %copy-start = (f32[160,1152]{1,0:T(8,128)S(1)}, f32[160,1152]{1,0:T(8,128)}, u32[]{:S(2)}) copy-start(f32[160,1152]{1,0:T(8,128)} %momentum.1) | copy-start | bytes 2211844

commit v7 on v6

--- a/solution.py
+++ b/solution.py
@@ -333,17 +333,17 @@
     settle(2)
     join(4)
     second(zr, 2)
+    spread(0)
     form(5)
     form(6)
-    spread(0)
     spread(1)
+    join(5)
     settle(3)
     spread(2)
+    join(6)
     first(zr, 3)
     form(7)
-    join(5)
     settle(4)
-    join(6)
     join(7)
 
     total = ss_z[0]
@@ -354,43 +354,43 @@
         small(ss_y, y, 0, at_y(wrap(y + d, Y))).start()
 
     meet(0)
+    meet(1)
     spread(3)
-    meet(1)
     settle(5)
+    meet(2)
+    settle(6)
     spread(4)
-    meet(2)
-    close(0)
-    settle(6)
-    close(1)
     settle(7)
+    spread(5)
     meet(3)
+    spread(6)
+    spread(7)
+    meet(4)
 
     landed(ss_y.at[pl.ds(0, 3)], ss_r.at[0])
     ss_x[x] = ss_y[0] + ss_y[1] + ss_y[2] + ss_y[3]
     for d in (1, 2, 3):
         small(ss_x, x, 1, at_x(wrap(x + d, X))).start()
 
-    spread(5)
+    close(0)
+    close(1)
     close(2)
-    meet(4)
-    spread(6)
-    spread(7)
-    close(3)
-
-    landed(ss_x.at[pl.ds(0, 3)], ss_r.at[1])
-    ss_c[core] = ss_x[0] + ss_x[1] + ss_x[2] + ss_x[3]
-    small(ss_c, core, 2, sibling).start()
-
-    close(4)
     meet(5)
     panel_wait(2)
     meet(6)
     meet(7)
+
+    landed(ss_x.at[pl.ds(0, 3)], ss_r.at[1])
+    ss_c[core] = ss_x[0] + ss_x[1] + ss_x[2] + ss_x[3]
+    small(ss_c, core, 2, sibling).start()
+
+    close(3)
+    close(4)
     multiply(0)
+    close(5)
     panel_wait(1)
     multiply(1)
     multiply(2)
-    close(5)
     close(6)
     multiply(3)
     close(7)

time: 112 us -> 110 us (0.982)
  Pallas kernels: 109 us -> 107 us
    pallas_call x1, Pallas kernels: 109 us -> 107 us  [fused(): pl.pallas_call(kernel, out_shape=(jax.ShapeDtypeStruct((ROWS, COLS), F32)...]
where the time goes in v7:
time: 110 us
  Pallas kernels  107 us (97%)
  other arithmetic  2.34 us (2%)
    pallas_call x1, Pallas kernels, fused(): pl.pallas_call(kernel, out_shape=(jax.ShapeDtypeStruct((ROWS, COLS), F32)...  107 us
    mul x1, other arithmetic, local(): update = (scale * product.reshape(ROWS // 8, 8, COLS)).reshape(ROWS, COLS)  2.34 us

profile of v7, /device:TPU:1, one launch (start us, length us, event | category | flops | bytes accessed | tf_op | source)
XLA Modules:
  0.0 110.2 jit_solution(5147614887462224466)
XLA Ops:
  0.6 0.0 copy-start.1
  0.6 0.0 copy-start
  0.6 107.2 %shard_map.41 = (f32[160,1152]{1,0:T(8,128)}, f32[8,1152]{1,0:T(8,128)}) custom-call(f32[160,1152]{1,0:T(8,128)} %momentum.1, bf16[160,1152]{1,0:T(8,128)(2,1)} %gradient.1), custom_call_target="tpu_custom_call" | custom-call | tf_op jit(solution)/shard_map/pallas_call | solution.py:570
  107.9 0.0 copy-done.1
  107.9 0.0 copy-done
  107.9 2.3 %bitcast_multiply_fusion = (f32[160,1152]{1,0:T(8,128)}, f32[160,1152]{1,0:T(8,128)}) fusion(f32[160,1152]{1,0:T(8,128)} %get-tuple-element.5, f32[8,1152]{1,0:T(8,128)} %get-tuple-element.4, bf16[160,1152]{1,0:T(8,128)(2,1)S(1)} %copy-done.1, f32[160,1152]{1,0:T(8,128)S(1)} %copy-done), kind=kLoop, calls=%fused_computation | loop fusion | flops 737280 | bytes 3354624 | tf_op jit(solution)/shard_map/mul | solution.py:622
Async XLA Ops:
  0.6 107.2 %copy-start.1 = (bf16[160,1152]{1,0:T(8,128)(2,1)S(1)}, bf16[160,1152]{1,0:T(8,128)(2,1)}, u32[]{:S(2)}) copy-start(bf16[160,1152]{1,0:T(8,128)(2,1)} %gradient.1) | copy-start | bytes 1105924
  0.6 107.2 %copy-start = (f32[160,1152]{1,0:T(8,128)S(1)}, f32[160,1152]{1,0:T(8,128)}, u32[]{:S(2)}) copy-start(f32[160,1152]{1,0:T(8,128)} %momentum.1) | copy-start | bytes 2211844

commit v8 on v7

--- a/solution.py
+++ b/solution.py
@@ -46,42 +46,35 @@
 
 
 class Ring:
-    def __init__(self, size, position, device, region, last, send_sem, recv_sems):
+    def __init__(self, size, position, device, region, whole, send_sem, recv_sems):
         self.size, self.position, self.device = size, position, device
-        self.region, self.last = region, last
+        self.region, self.whole = region, whole
         self.send_sem, self.recv_sems = send_sem, recv_sems
-        self.slots = {}
+
+    def send(self, kind, step):
         for way in (0, 1):
-            for piece in range(len(last)):
-                for step in range(size // 2 - (0 if last[piece] == way else 1)):
-                    self.slots[way, step, piece] = len(self.slots)
-
-    def copy(self, way, step, piece, block):
-        sign = 1 - 2 * way
-        place = self.region(block, piece)
-        return remote(
-            place,
-            place,
-            self.send_sem,
-            self.recv_sems.at[self.slots[way, step, piece]],
-            self.device(wrap(self.position + sign, self.size)),
-        )
-
-    def send(self, way, step, piece):
-        sign = 1 - 2 * way
-        self.copy(way, step, piece, wrap(self.position - sign * step, self.size)).start()
+            sign = 1 - 2 * way
+            place = self.region(
+                wrap(self.position - sign * step, self.size), way if kind == 0 else 1 - way
+            )
+            remote(
+                place,
+                place,
+                self.send_sem,
+                self.recv_sems.at[2 * step + kind],
+                self.device(wrap(self.position + sign, self.size)),
+            ).start()
 
     def start(self):
-        for way, piece in ((0, 0), (1, 1), (0, 1), (1, 0)):
-            self.send(way, 0, piece)
-
-    def recv(self, way, step, piece):
-        if (way, step, piece) not in self.slots:
-            return
-        sign = 1 - 2 * way
-        self.copy(way, step, piece, wrap(self.position - sign * (step + 1), self.size)).wait_recv()
-        if (way, step + 1, piece) in self.slots:
-            self.send(way, step + 1, piece)
+        self.send(0, 0)
+        self.send(1, 0)
+
+    def recv(self, kind, step):
+        remote(
+            self.whole, self.whole, self.send_sem, self.recv_sems.at[2 * step + kind], self.device(self.position)
+        ).wait_recv()
+        if step + 1 < self.size // 2 - kind:
+            self.send(kind, step + 1)
 
 
 OFFSETS = (0, 1, -1, 2, -2, 3, -3, 4)
@@ -92,7 +85,7 @@
     gradient,
     product,
     factor_out,
-    xa, xb, part, sibling_part, units, gj, gall, pb, up, y_relay, y_last, uz, z_sum,
+    momentum_here, gradient_here, load_sems, xa, xb, part, sibling_part, units, gj, gall, pb, up, y_relay, y_last, uz, z_sum,
     square, ss_z, ss_y, ss_x, ss_c,
     sent, zr_r, yr_r, sp_r, us_r, gz_r, gt_r, gy_r, gs_r, pr_r, ps_r, ss_r, ur_r, ul_r, zs_r,
 ):
@@ -118,16 +111,24 @@
     partners += [at_x(wrap(x + d, X)) for d in (1, 2, 3)]
     for partner in partners:
         pl.semaphore_signal(barrier, inc=1, device_id=partner, device_id_type=pl.DeviceIdType.MESH)
-    iterate = (decay_rate * momentum[...] + gradient[...].astype(F32)).astype(BF16)
+    loads = [
+        pltpu.make_async_copy(momentum, momentum_here, load_sems.at[0]),
+        pltpu.make_async_copy(gradient, gradient_here, load_sems.at[1]),
+    ]
+    for copy in loads:
+        copy.start()
+    for copy in loads:
+        copy.wait()
+    iterate = (decay_rate * momentum_here[...] + gradient_here[...].astype(F32)).astype(BF16)
     xb[z] = iterate
     xa[y] = iterate
     pl.semaphore_wait(barrier, len(partners))
 
-    zr = Ring(Z, z, at_z, lambda b, p: xb.at[b, pl.ds(p * HALF, HALF)], (0, 1), sent.at[0], zr_r)
-    yr = Ring(Y, y, at_y, lambda b, p: xa.at[b, pl.ds(p * HALF, HALF)], (0, 1), sent.at[1], yr_r)
-    for way, piece in ((0, 0), (1, 1), (0, 1), (1, 0)):
-        zr.send(way, 0, piece)
-        yr.send(way, 0, piece)
+    zr = Ring(Z, z, at_z, lambda b, p: xb.at[b, pl.ds(p * HALF, HALF)], xb.at[0], sent.at[0], zr_r)
+    yr = Ring(Y, y, at_y, lambda b, p: xa.at[b, pl.ds(p * HALF, HALF)], xa.at[0], sent.at[1], yr_r)
+    for kind in (0, 1):
+        zr.send(kind, 0)
+        yr.send(kind, 0)
 
     def z_of(event):
         return wrap(z + OFFSETS[event], Z)
@@ -191,21 +192,36 @@
             place, place, sent.at[4], gz_r.at[slot], at_z(wrap(z + (1 - 2 * way) * hops, Z))
         )
 
-    def panel_start(piece):
+    def panel_start(piece, late):
         for hops in (2, 1):
             for way in (0, 1):
-                panel_copy(way, hops, z, 4 * (hops - 1) + 2 * way + piece, piece).start()
+                slot = 0 if hops == 1 else 4 + 2 * way + late
+                panel_copy(way, hops, z, slot, piece).start()
+
+    def panel_on(late):
+        for way in (0, 1):
+            block = wrap(z - (1 - 2 * way) * 2, Z)
+            near = lax.div(wrap(wrap(x - block, Z) + 1 - Z, Z), X)
+            middle = wrap(wrap(x - block, Z) - Z, X) == 2
+
+            def go(piece, slot):
+                landed(gj.at[0, 0], gz_r.at[slot])
+
+                @pl.when(piece == way)
+                def _():
+                    panel_copy(way, 2, block, 3, piece).start()
+
+                panel_copy(way, 1, block, 2, piece).start()
+
+            @pl.when(middle if late else jnp.logical_not(middle))
+            def _():
+                go(near, 4 + 2 * way)
+
+            if late:
+                go(1 - near, 5 + 2 * way)
 
     def panel_wait(distance):
-        for way in (0, 1):
-            for piece in (0, 1) if distance < 4 else (way,):
-                slot = 4 * (distance - 1) + (2 * way + piece if distance < 4 else way)
-                block = wrap(z - (1 - 2 * way) * distance, Z)
-                panel_copy(way, 1, block, slot, piece).wait_recv()
-                if distance == 2:
-                    if piece == way:
-                        panel_copy(way, 2, block, 12 + way, piece).start()
-                    panel_copy(way, 1, block, 8 + 2 * way + piece, piece).start()
+        landed(gj.at[pl.ds(0, 2)] if distance < 4 else gj.at[0], gz_r.at[distance - 1])
 
     gy = []
     for event in range(Z):
@@ -216,7 +232,7 @@
                 y,
                 at_y,
                 lambda b, p, there=there: gall.at[there, b, core, pl.ds(*cut[p])],
-                (0, 1),
+                gall.at[there, 0, core],
                 sent.at[6],
                 gy_r.at[there],
             )
@@ -279,17 +295,16 @@
         def _():
             half = lax.div(there, X)
             gj[z, half] = gall[there, y, core]
-            panel_start(half)
+            panel_start(half, 0 if event < 4 else 1)
 
     def meet(event):
-        for way, piece in ((0, 0), (1, 1), (0, 1), (1, 0)):
-            gy[event].recv(way, 0, piece)
+        gy[event].recv(0, 0)
+        gy[event].recv(1, 0)
         share(z_of(event), 1, core).start()
         share(z_of(event), 3, core).start()
 
     def close(event):
-        gy[event].recv(0, 1, 0)
-        gy[event].recv(1, 1, 1)
+        gy[event].recv(0, 1)
         share(z_of(event), 2, core).start()
 
     def multiply(event):
@@ -300,12 +315,10 @@
         )
 
     def first(ring, step):
-        ring.recv(0, step, 0)
-        ring.recv(1, step, 1)
+        ring.recv(0, step)
 
     def second(ring, step):
-        ring.recv(0, step, 1)
-        ring.recv(1, step, 0)
+        ring.recv(1, step)
 
     def small(refs, slot, index, device):
         return remote(refs.at[slot], refs.at[slot], sent.at[10 + index], ss_r.at[index], device)
@@ -360,6 +373,7 @@
     meet(2)
     settle(6)
     spread(4)
+    panel_on(False)
     settle(7)
     spread(5)
     meet(3)
@@ -376,7 +390,7 @@
     close(1)
     close(2)
     meet(5)
-    panel_wait(2)
+    panel_on(True)
     meet(6)
     meet(7)
 
@@ -405,7 +419,7 @@
     panel_wait(4)
     multiply(7)
 
-    pr = Ring(X, x, at_x, lambda b, p: pb.at[p, b, core], (0, 1), sent.at[8], pr_r)
+    pr = Ring(X, x, at_x, lambda b, p: pb.at[p, b, core], pb.at[:, 0, core], sent.at[8], pr_r)
     for half in (0, 1):
         gram = gj[z, half].astype(F32)
         tile = (
@@ -424,7 +438,7 @@
             up.at[tile, wrap(y + 2, Y), pl.ds(side * HALF, HALF)],
             y_relay.at[tile, side],
             sent.at[13],
-            ur_r.at[tile, side],
+            ur_r.at[tile],
             at_y(wrap(y + 1 - 2 * side, Y)),
         )
 
@@ -433,13 +447,13 @@
             up.at[tile, wrap(y + 1 - 2 * side, Y), pl.ds(half * HALF, HALF)],
             y_last.at[tile, side, pl.ds(half * HALF, HALF)],
             sent.at[14],
-            ul_r.at[tile, side, half],
+            ul_r.at[tile],
             at_y(wrap(y + 1 - 2 * side, Y)),
         )
 
     def add_relay(tile):
+        landed(y_relay.at[tile], ur_r.at[tile])
         for side in (0, 1):
-            y_relay_copy(tile, side).wait_recv()
             near = wrap(y + 1 - 2 * side, Y)
             place = pl.ds(side * HALF, HALF)
             up[tile, near, place] = up[tile, near, place] + y_relay[tile, side]
@@ -451,14 +465,14 @@
             uz.at[wrap(z + sign * (4 - step), Z), pl.ds(half * HALF, HALF)],
             z_sum.at[way, step, half],
             sent.at[15],
-            zs_r.at[way, step, half],
+            zs_r.at[2 * step + (half + way) % 2],
             at_z(wrap(z + sign, Z)),
         )
 
     def z_sum_step(step, second_half):
+        landed(z_sum.at[0, 0], zs_r.at[2 * step + second_half])
         for way in (0, 1):
             half = way if not second_half else 1 - way
-            z_sum_copy(way, step, half).wait_recv()
             near = wrap(z + (1 - 2 * way) * (3 - step), Z)
             place = pl.ds(half * HALF, HALF)
             uz[near, place] = uz[near, place] + z_sum[way, step, half]
@@ -496,17 +510,16 @@
             y_last_copy(tile, side, 1 - side).start()
 
     def finish_y(tile):
-        for side in (0, 1):
-            for half in (0, 1):
-                y_last_copy(tile, side, half).wait_recv()
+        landed(y_last.at[tile], ul_r.at[tile])
         columns = pl.ds(tile * TILE, TILE)
         product[:, columns] = (
             linear_coef * xb[z, :, columns].astype(F32) + up[tile, y] + y_last[tile, 0] + y_last[tile, 1]
         )
 
     def finish_z(half):
-        for way in (0, 1):
-            z_sum_copy(way, 3, half).wait_recv()
+        if half == 0:
+            landed(z_sum.at[0, 0], zs_r.at[6])
+            landed(z_sum.at[0, 0], zs_r.at[7])
         rows, columns = pl.ds(half * HALF, HALF), pl.ds(SPLIT, TILE)
         product[rows, columns] = (
             linear_coef * xb[z, rows, columns].astype(F32)
@@ -573,9 +586,12 @@
             jax.ShapeDtypeStruct((ROWS, COLS), F32),
             jax.ShapeDtypeStruct((8, COLS), F32),
         ),
-        in_specs=[vmem, vmem],
+        in_specs=[pl.BlockSpec(memory_space=pl.ANY)] * 2,
         out_specs=(vmem, vmem),
         scratch_shapes=[
+            pltpu.VMEM((ROWS, COLS), F32),
+            pltpu.VMEM((ROWS, COLS), BF16),
+            dma(2),
             pltpu.VMEM((Y, ROWS, COLS), BF16),
             pltpu.VMEM((Z, ROWS, COLS), BF16),
             pltpu.VMEM((Z, 2, HALF, WIDE), F32),
@@ -595,20 +611,20 @@
             pltpu.VMEM((X, 8, 128), F32),
             pltpu.VMEM((2, 8, 128), F32),
             dma(16),
-            dma(14),
-            dma(6),
+            dma(7),
+            dma(3),
             dma(Z),
             dma(Z),
-            dma(14),
+            dma(8),
             dma(Z),
-            dma(Z, 6),
+            dma(Z, 3),
             dma(Z),
-            dma(6),
+            dma(3),
             dma(X),
             dma(3),
-            dma(TILES, 2),
-            dma(TILES, 2, 2),
-            dma(2, 4, 2),
+            dma(TILES),
+            dma(TILES),
+            dma(8),
         ],
         compiler_params=pltpu.CompilerParams(
             collective_id=0, has_side_effects=True, vmem_limit_bytes=56 * 1024 * 1024

time: 110 us -> 109 us (level)
    pallas_call x1, Pallas kernels: 107 us -> 106 us  [fused(): pl.pallas_call(kernel, out_shape=(jax.ShapeDtypeStruct((ROWS, COLS), F32)...]
where the time goes in v8:
time: 109 us
  Pallas kernels  106 us (97%)
  other arithmetic  2.34 us (2%)
    pallas_call x1, Pallas kernels, fused(): pl.pallas_call(kernel, out_shape=(jax.ShapeDtypeStruct((ROWS, COLS), F32)...  106 us
    mul x1, other arithmetic, local(): update = (scale * product.reshape(ROWS // 8, 8, COLS)).reshape(ROWS, COLS)  2.34 us

profile of v8, /device:TPU:1, one launch (start us, length us, event | category | flops | bytes accessed | tf_op | source)
XLA Modules:
  0.0 109.0 jit_solution(5352095085744775616)
XLA Ops:
  0.6 0.0 copy-start.1
  0.6 0.0 copy-start
  0.6 106.0 %shard_map.41 = (f32[160,1152]{1,0:T(8,128)}, f32[8,1152]{1,0:T(8,128)}) custom-call(f32[160,1152]{1,0:T(8,128)} %momentum.1, bf16[160,1152]{1,0:T(8,128)(2,1)} %gradient.1), custom_call_target="tpu_custom_call" | custom-call | tf_op jit(solution)/shard_map/pallas_call | solution.py:583
  106.6 0.0 copy-done.1
  106.6 0.0 copy-done
  106.6 2.3 %bitcast_multiply_fusion = (f32[160,1152]{1,0:T(8,128)}, f32[160,1152]{1,0:T(8,128)}) fusion(f32[160,1152]{1,0:T(8,128)} %get-tuple-element.5, f32[8,1152]{1,0:T(8,128)} %get-tuple-element.4, bf16[160,1152]{1,0:T(8,128)(2,1)S(1)} %copy-done.1, f32[160,1152]{1,0:T(8,128)S(1)} %copy-done), kind=kLoop, calls=%fused_computation | loop fusion | flops 737280 | bytes 3354624 | tf_op jit(solution)/shard_map/mul | solution.py:638
Async XLA Ops:
  0.6 106.0 %copy-start.1 = (bf16[160,1152]{1,0:T(8,128)(2,1)S(1)}, bf16[160,1152]{1,0:T(8,128)(2,1)}, u32[]{:S(2)}) copy-start(bf16[160,1152]{1,0:T(8,128)(2,1)} %gradient.1) | copy-start | bytes 1105924
  0.6 106.0 %copy-start = (f32[160,1152]{1,0:T(8,128)S(1)}, f32[160,1152]{1,0:T(8,128)}, u32[]{:S(2)}) copy-start(f32[160,1152]{1,0:T(8,128)} %momentum.1) | copy-start | bytes 2211844

commit v9 on v8

--- a/solution.py
+++ b/solution.py
@@ -83,8 +83,7 @@
 def kernel(
     momentum,
     gradient,
-    product,
-    factor_out,
+    update,
     momentum_here, gradient_here, load_sems, xa, xb, part, sibling_part, units, gj, gall, pb, up, y_relay, y_last, uz, z_sum,
     square, ss_z, ss_y, ss_x, ss_c,
     sent, zr_r, yr_r, sp_r, us_r, gz_r, gt_r, gy_r, gs_r, pr_r, ps_r, ss_r, ur_r, ul_r, zs_r,
@@ -177,7 +176,7 @@
         there = z_of(event)
         sibling_copy(there).wait_recv()
         part[there, core] = part[there, core] + sibling_part[there]
-        for d in (2, 1, 3):
+        for d in (1, 3, 2):
             unit_copy(there, d).start()
         role = role_of(there)
 
@@ -260,7 +259,7 @@
             gall[there, y, core, EXTRA] = (
                 part[there, core, EXTRA] + units[there, 3] + units[there, 4] + units[there, 5]
             ).astype(BF16)
-            for d in (2, 1, 3):
+            for d in (1, 3, 2):
                 extra_tile_copy(there, d).start()
 
         @pl.when(role != 0)
@@ -270,7 +269,7 @@
         gall[there, y, core, rows] = (
             part[there, core, rows] + units[there, 0] + units[there, 1] + units[there, 2]
         ).astype(BF16)
-        for d in (2, 1, 3):
+        for d in (1, 3, 2):
             tile_copy(there, d).start()
 
     def share(there, k, core_):
@@ -335,8 +334,8 @@
     join(0)
     form(2)
     join(1)
+    second(zr, 1)
     join(2)
-    second(zr, 1)
     form(3)
     form(4)
     settle(0)
@@ -412,7 +411,7 @@
     small(ss_c, other, 2, sibling).wait_recv()
     norm_total = (ss_c[0] + ss_c[1])[0:1, 0:1]
     factor = math.sqrt(FULL_ROWS) / (3.0 * (jnp.sqrt(norm_total) + norm_eps))
-    factor_out[...] = jnp.broadcast_to(math.sqrt(FULL_COLS) * factor, factor_out.shape)
+    scale = math.sqrt(FULL_COLS) * factor
     panel_wait(3)
     multiply(5)
     multiply(6)
@@ -512,7 +511,7 @@
     def finish_y(tile):
         landed(y_last.at[tile], ul_r.at[tile])
         columns = pl.ds(tile * TILE, TILE)
-        product[:, columns] = (
+        update[:, columns] = scale * (
             linear_coef * xb[z, :, columns].astype(F32) + up[tile, y] + y_last[tile, 0] + y_last[tile, 1]
         )
 
@@ -521,7 +520,7 @@
             landed(z_sum.at[0, 0], zs_r.at[6])
             landed(z_sum.at[0, 0], zs_r.at[7])
         rows, columns = pl.ds(half * HALF, HALF), pl.ds(SPLIT, TILE)
-        product[rows, columns] = (
+        update[rows, columns] = scale * (
             linear_coef * xb[z, rows, columns].astype(F32)
             + uz[z, rows]
             + z_sum[0, 3, half]
@@ -534,9 +533,9 @@
     second(pr, 0)
     share_p(1, core).start()
     share_p(3, core).start()
-    grow(1)
     first(pr, 1)
     share_p(2, core).start()
+    grow(1)
     grow(3)
     grow(2)
     begin_near(0)
@@ -582,12 +581,9 @@
     vmem = pl.BlockSpec(memory_space=pltpu.VMEM)
     return pl.pallas_call(
         kernel,
-        out_shape=(
-            jax.ShapeDtypeStruct((ROWS, COLS), F32),
-            jax.ShapeDtypeStruct((8, COLS), F32),
-        ),
+        out_shape=jax.ShapeDtypeStruct((ROWS, COLS), F32),
         in_specs=[pl.BlockSpec(memory_space=pl.ANY)] * 2,
-        out_specs=(vmem, vmem),
+        out_specs=vmem,
         scratch_shapes=[
             pltpu.VMEM((ROWS, COLS), F32),
             pltpu.VMEM((ROWS, COLS), BF16),
@@ -634,8 +630,7 @@
 
 def local(momentum, gradient):
     new_momentum = decay_rate * momentum + gradient.astype(F32)
-    product, scale = fused(momentum, gradient)
-    update = (scale * product.reshape(ROWS // 8, 8, COLS)).reshape(ROWS, COLS)
+    update = fused(momentum, gradient)
     return (new_momentum, update)
 
 

time: 109 us -> 108 us (level)
  other arithmetic: 2.34 us -> 0.94 us
  local copies, waits for them, and re-layouts: 0.01 us -> 1.31 us
    mul x1 -> x0, other arithmetic: 2.34 us -> none  [local(): update = (scale * product.reshape(ROWS // 8, 8, COLS)).reshape(ROWS, COLS)]
    pallas_call x1, Pallas kernels: 106 us -> 105 us  [fused(): pl.pallas_call(kernel, out_shape=jax.ShapeDtypeStruct((ROWS, COLS), F32),...]
    unnamed x4 -> x7, local copies, waits for them, and re-layouts: 0.01 us -> 1.31 us
where the time goes in v9:
time: 108 us
  Pallas kernels  105 us (97%)
  local copies, waits for them, and re-layouts  1.31 us (1%)
    pallas_call x1, Pallas kernels, fused(): pl.pallas_call(kernel, out_shape=jax.ShapeDtypeStruct((ROWS, COLS), F32),...  105 us

profile of v9, /device:TPU:1, one launch (start us, length us, event | category | flops | bytes accessed | tf_op | source)
XLA Modules:
  0.0 107.6 jit_solution(12753964467170413122)
XLA Ops:
  0.6 0.0 copy-start.2
  0.6 0.0 copy-start
  0.6 104.7 %shard_map.41 = f32[160,1152]{1,0:T(8,128)} custom-call(f32[160,1152]{1,0:T(8,128)} %momentum.1, bf16[160,1152]{1,0:T(8,128)(2,1)} %gradient.1), custom_call_target="tpu_custom_call" | custom-call | tf_op jit(solution)/shard_map/pallas_call | solution.py:582
  105.3 0.0 copy-done.2
  105.3 0.0 copy-done
  105.3 0.0 copy-start.1
  105.3 0.9 convert_add_fusion
  106.3 0.4 copy-done.1
  106.7 0.9 copy.5
Async XLA Ops:
  0.6 104.7 %copy-start.2 = (bf16[160,1152]{1,0:T(8,128)(2,1)S(1)}, bf16[160,1152]{1,0:T(8,128)(2,1)}, u32[]{:S(2)}) copy-start(bf16[160,1152]{1,0:T(8,128)(2,1)} %gradient.1) | copy-start | bytes 1105924
  0.6 104.7 %copy-start = (f32[160,1152]{1,0:T(8,128)S(1)}, f32[160,1152]{1,0:T(8,128)}, u32[]{:S(2)}) copy-start(f32[160,1152]{1,0:T(8,128)} %momentum.1) | copy-start | bytes 2211844
  105.3 1.4 %copy-start.1 = (f32[160,1152]{1,0:T(8,128)S(1)}, f32[160,1152]{1,0:T(8,128)}, u32[]{:S(2)}) copy-start(f32[160,1152]{1,0:T(8,128)} %shard_map.41) | copy-start | bytes 2211844

commit v10 on v9

--- a/solution.py
+++ b/solution.py
@@ -201,7 +201,6 @@
         for way in (0, 1):
             block = wrap(z - (1 - 2 * way) * 2, Z)
             near = lax.div(wrap(wrap(x - block, Z) + 1 - Z, Z), X)
-            middle = wrap(wrap(x - block, Z) - Z, X) == 2
 
             def go(piece, slot):
                 landed(gj.at[0, 0], gz_r.at[slot])
@@ -212,12 +211,10 @@
 
                 panel_copy(way, 1, block, 2, piece).start()
 
-            @pl.when(middle if late else jnp.logical_not(middle))
-            def _():
-                go(near, 4 + 2 * way)
-
             if late:
                 go(1 - near, 5 + 2 * way)
+            else:
+                go(near, 4 + 2 * way)
 
     def panel_wait(distance):
         landed(gj.at[pl.ds(0, 2)] if distance < 4 else gj.at[0], gz_r.at[distance - 1])

time: 108 us -> 109 us (level)
  no operation moved by 1% of the time
where the time goes in v10:
time: 109 us; the launch traced here: 108 us
  Pallas kernels  105 us (96%)
  local copies, waits for them, and re-layouts  1.31 us (1%)
    pallas_call x1, Pallas kernels, fused(): pl.pallas_call(kernel, out_shape=jax.ShapeDtypeStruct((ROWS, COLS), F32),...  105 us

profile of v10, /device:TPU:1, one launch (start us, length us, event | category | flops | bytes accessed | tf_op | source)
XLA Modules:
  0.0 108.1 jit_solution(2661046590783419761)
XLA Ops:
  0.6 0.0 copy-start.2
  0.6 0.0 copy-start
  0.6 105.2 %shard_map.41 = f32[160,1152]{1,0:T(8,128)} custom-call(f32[160,1152]{1,0:T(8,128)} %momentum.1, bf16[160,1152]{1,0:T(8,128)(2,1)} %gradient.1), custom_call_target="tpu_custom_call" | custom-call | tf_op jit(solution)/shard_map/pallas_call | solution.py:579
  105.8 0.0 copy-done.2
  105.8 0.0 copy-done
  105.8 0.0 copy-start.1
  105.8 0.9 convert_add_fusion
  106.8 0.4 copy-done.1
  107.2 0.9 copy.5
Async XLA Ops:
  0.6 105.2 %copy-start.2 = (bf16[160,1152]{1,0:T(8,128)(2,1)S(1)}, bf16[160,1152]{1,0:T(8,128)(2,1)}, u32[]{:S(2)}) copy-start(bf16[160,1152]{1,0:T(8,128)(2,1)} %gradient.1) | copy-start | bytes 1105924
  0.6 105.2 %copy-start = (f32[160,1152]{1,0:T(8,128)S(1)}, f32[160,1152]{1,0:T(8,128)}, u32[]{:S(2)}) copy-start(f32[160,1152]{1,0:T(8,128)} %momentum.1) | copy-start | bytes 2211844
  105.8 1.4 %copy-start.1 = (f32[160,1152]{1,0:T(8,128)S(1)}, f32[160,1152]{1,0:T(8,128)}, u32[]{:S(2)}) copy-start(f32[160,1152]{1,0:T(8,128)} %shard_map.41) | copy-start | bytes 2211844
